TPU v7x, 128 devices: a whole 4x4x4 slice. The times are simulated.
128 devices in a mesh: layer: 4 (over x), energy: 32 (over y, z, core).
Axes of the slice: x: 4, y: 4, z: 4, core: 2. Of those that a mesh axis runs over, the one named last changes fastest.
Arguments:
- onsite: float32 [4, 256], P('layer'), may hold values from -1 to 1
- broadening: float32 [4, 256], P('layer'), may hold values from 1 to 2
- hamiltonian: float32 [4, 2, 256, 256], P('layer'), may hold values from -0.078125 to 0.078125
- coupling: float32 [4, 2, 256, 256], P('layer'), may hold values from -0.21875 to 0.21875
- coupling_mask: int32 [4, 256, 256], P('layer'), may hold values 0 or 1
- prior_sigma: float32 [4, 128, 2, 256, 256], P('layer', 'energy'), may hold values from -0.4 to 0.4, as said below
- kernel_weights: float32 [8], replicated, may hold values from 0.1 to 0.6
- kernel_offsets: int32 [8], replicated, may hold values from -7 to 7
Outputs:
- self_energy: float32 [4, 128, 2, 256, 256], P('layer', 'energy')
Inputs may be any that keep to these rules, and one draw needn't show every extreme that they name: `prior_sigma`: real and imaginary parts of the blocks.
All inputs are finite; a program needn't handle non-finite values. No bound on the sum of `coupling_mask` on one device may be relied on, other than what follows from the above.
Results may differ from a plain program's by a relative error of at most 0.0001.
Values sent between devices are 32-bit elements; how exact they have to be, the bound alone decides.
A program may use at most 128 MiB of HBM per device.

v0:
```python
import jax
import jax.numpy as jnp
from jax import lax
from jax.sharding import PartitionSpec as P

NS_ITERS = 3


exact_mode = lax.Precision.HIGHEST


def from_behind(block, axis, distance):
    devices = range(lax.axis_size(axis))
    route = [(i - distance, i) for i in devices if i - distance in devices]
    return lax.ppermute(block, axis, route)


def matmul_high(first_op, second_op):
    return jnp.matmul(first_op, second_op, precision=exact_mode)


def complex_product(first_op, second_op):
    first_real = first_op[..., 0, :, :]
    first_imag = first_op[..., 1, :, :]
    second_real = second_op[..., 0, :, :]
    second_imag = second_op[..., 1, :, :]
    real_part = matmul_high(first_real, second_real) - matmul_high(first_imag, second_imag)
    imag_part = matmul_high(first_real, second_imag) + matmul_high(first_imag, second_real)
    return jnp.stack([real_part, imag_part], axis=-3)


def adjoint(matrix):
    return jnp.stack(
        [jnp.swapaxes(matrix[..., 0, :, :], -1, -2), -jnp.swapaxes(matrix[..., 1, :, :], -1, -2)],
        axis=-3,
    )


def lead_block(batch_size, orbitals):
    identity = jnp.eye(orbitals, dtype=jnp.float32)
    single = jnp.stack([jnp.zeros_like(identity), -0.5 * identity])
    return jnp.broadcast_to(single, (batch_size, 2, orbitals, orbitals))


def energy_levels(positions, grid_size):
    return -1.0 + 2.0 * (positions.astype(jnp.float32) + 0.5) / grid_size


def solve_layer(
    levels, onsite_row, damping_row, hamilton, coupler, pattern, previous, incoming, sweeps
):
    orbitals = hamilton.shape[-1]
    identity = jnp.eye(orbitals, dtype=jnp.float32)
    hermitian = 0.5 * (hamilton + adjoint(hamilton))
    masked = coupler * pattern.astype(jnp.float32)[None]
    contact = complex_product(complex_product(masked[None], incoming), adjoint(masked)[None])
    real_diag = levels[:, None] - onsite_row[None, :]
    imag_diag = damping_row[None, :]
    shifted = jnp.stack([real_diag, imag_diag], axis=1)[..., None, :] * identity
    system = shifted - hermitian[None] - contact - previous
    diag_real = jnp.diagonal(system[:, 0], axis1=-2, axis2=-1)
    diag_imag = jnp.diagonal(system[:, 1], axis1=-2, axis2=-1)
    modulus = diag_real * diag_real + diag_imag * diag_imag
    inverse = (
        jnp.stack([diag_real / modulus, -diag_imag / modulus], axis=1)[..., None, :] * identity
    )
    for sweep_no in range(sweeps):
        residue = complex_product(system, inverse)
        inverse = 2.0 * inverse - complex_product(inverse, residue)
    return inverse


def convolution_matrix(weights, offsets, row_count, col_count):
    row_idx = jnp.arange(row_count, dtype=jnp.int32)
    col_idx = jnp.arange(col_count, dtype=jnp.int32)
    matches = col_idx[None, None, :] == row_idx[None, :, None] + offsets[:, None, None]
    return jnp.sum(jnp.where(matches, weights[:, None, None], jnp.float32(0.0)), axis=0)


def local(
    onsite,
    broadening,
    hamiltonian,
    coupling,
    coupling_mask,
    prior_sigma,
    kernel_weights,
    kernel_offsets,
):
    layer_count = lax.axis_size("layer")
    group_count = lax.axis_size("energy")
    per_device = prior_sigma.shape[1]
    orbitals = prior_sigma.shape[-1]
    grid_size = per_device * group_count
    first_level = lax.axis_index("energy") * per_device
    own_levels = energy_levels(first_level + jnp.arange(per_device, dtype=jnp.int32), grid_size)
    position = lax.axis_index("layer")
    batch_size = per_device // layer_count
    entry_block = lead_block(batch_size, orbitals)
    incoming = jnp.zeros_like(entry_block)
    green_blocks = jnp.zeros((per_device, 2, orbitals, orbitals), jnp.float32)
    step_total = layer_count + layer_count - 1
    for step_no in range(step_total):
        batch_no = step_no - position
        active = jnp.logical_and(batch_no >= 0, batch_no < layer_count)
        offset_row = jnp.clip(batch_no, 0, layer_count - 1) * batch_size
        entering = jnp.where(position == 0, entry_block, incoming)

        def advance(operands):
            row_start, arriving = operands
            levels_now = lax.dynamic_slice_in_dim(own_levels, row_start, batch_size, 0)
            prior_now = lax.dynamic_slice_in_dim(prior_sigma[0], row_start, batch_size, 0)
            return solve_layer(
                levels_now,
                onsite[0],
                broadening[0],
                hamiltonian[0],
                coupling[0],
                coupling_mask[0],
                prior_now,
                arriving,
                NS_ITERS,
            )

        def resting(operands):
            return jnp.zeros_like(operands[1])

        result_block = lax.cond(active, advance, resting, (offset_row, entering))
        current = lax.dynamic_slice_in_dim(green_blocks, offset_row, batch_size, 0)
        green_blocks = lax.dynamic_update_slice_in_dim(
            green_blocks, jnp.where(active, result_block, current), offset_row, 0
        )
        if step_no + 1 < step_total:
            incoming = from_behind(result_block, "layer", 1)
    kernel = convolution_matrix(kernel_weights, kernel_offsets, grid_size, grid_size)
    blended = jnp.einsum(
        "fe,epij->fpij",
        kernel,
        lax.all_to_all(green_blocks, "energy", split_axis=2, concat_axis=0, tiled=True),
        precision=exact_mode,
    )
    scattering = lax.all_to_all(blended, "energy", split_axis=0, concat_axis=2, tiled=True)
    return scattering[None]


def solution(mesh):
    placed = (
        P("layer", None),
        P("layer", None),
        P("layer", None, None, None),
        P("layer", None, None, None),
        P("layer", None, None),
        P("layer", "energy", None, None, None),
        P(),
        P(),
    )
    return jax.shard_map(
        local,
        mesh=mesh,
        in_specs=placed,
        out_specs=P("layer", "energy", None, None, None),
        check_vma=False,
    )
```

profile of v0, /device:TPU:30, one launch (start us, length us, event | category | flops | bytes accessed | tf_op | source)
XLA Modules:
  0.0 340.7 jit_solution(1518905506484917890)
XLA Ops:
  0.1 3.7 %conditional.7 = (f32[1,2,256,256]{3,2,1,0:T(8,128)S(1)}) conditional(s32[]{:T(128)} %convert_element_type.116, () %tuple.47, (s32[]{:T(128)}, f32[4]{0:T(128)S(1)}, f32[1,256]{1,0:T(1,128)}, f32[1,256]{1,0:T(1,128)}, f32[1,2,256,256]{3,2,1,0:T(8,128)}, /*index=5*/s32[1,256,256]{2,1,0:T(8,128)}, f32[1,2,256,256]{3,2,1,0:T(8,128)}, pred[]{:T(512)}, ...), branch_computations={%region_1.2_spmd, %region_2.3_spmd} | conditional | flops 6448287744 | bytes 52475052 | solution.py:128
  5.1 14.2 %collective-permute-done = f32[1,2,256,256]{3,2,1,0:T(8,128)S(1)} collective-permute-done((f32[1,2,256,256]{3,2,1,0:T(8,128)S(1)}, f32[1,2,256,256]{3,2,1,0:T(8,128)S(1)}, u32[]{:S(2)}, u32[]{:S(2)}) %collective-permute-start) | collective-permute-done | bytes 524320 | tf_op jit(solution)/shard_map/ppermute | solution.py:15
  19.4 3.9 %conditional.8 = (f32[1,2,256,256]{3,2,1,0:T(8,128)S(1)}) conditional(s32[]{:T(128)} %convert_element_type.118, () %tuple.49, (s32[]{:T(128)}, f32[4]{0:T(128)S(1)}, f32[1,256]{1,0:T(1,128)}, f32[1,256]{1,0:T(1,128)}, f32[1,2,256,256]{3,2,1,0:T(8,128)}, /*index=5*/s32[1,256,256]{2,1,0:T(8,128)}, f32[1,2,256,256]{3,2,1,0:T(8,128)}, pred[]{:T(512)}, ...), branch_computations={%region_3.4_spmd, %region_4.5_spmd} | conditional | flops 6448287744 | bytes 52999340 | solution.py:128
  24.6 13.4 %collective-permute-done.1 = f32[1,2,256,256]{3,2,1,0:T(8,128)S(1)} collective-permute-done((f32[1,2,256,256]{3,2,1,0:T(8,128)S(1)}, f32[1,2,256,256]{3,2,1,0:T(8,128)S(1)}, u32[]{:S(2)}, u32[]{:S(2)}) %collective-permute-start.1) | collective-permute-done | bytes 524320 | tf_op jit(solution)/shard_map/ppermute | solution.py:15
  38.0 3.6 %conditional.9 = (f32[1,2,256,256]{3,2,1,0:T(8,128)S(1)}) conditional(s32[]{:T(128)} %convert_element_type.119, () %tuple.51, (s32[]{:T(128)}, f32[4]{0:T(128)S(1)}, f32[1,256]{1,0:T(1,128)}, f32[1,256]{1,0:T(1,128)}, f32[1,2,256,256]{3,2,1,0:T(8,128)}, /*index=5*/s32[1,256,256]{2,1,0:T(8,128)}, f32[1,2,256,256]{3,2,1,0:T(8,128)}, pred[]{:T(512)}, ...), branch_computations={%region_5.6_spmd, %region_6.7_spmd} | conditional | flops 6448287744 | bytes 52999340 | solution.py:128
  42.9 68.8 %collective-permute-done.2 = f32[1,2,256,256]{3,2,1,0:T(8,128)S(1)} collective-permute-done((f32[1,2,256,256]{3,2,1,0:T(8,128)S(1)}, f32[1,2,256,256]{3,2,1,0:T(8,128)S(1)}, u32[]{:S(2)}, u32[]{:S(2)}) %collective-permute-start.2) | collective-permute-done | bytes 524320 | tf_op jit(solution)/shard_map/ppermute | solution.py:15
  111.7 41.6 %conditional.10 = (f32[1,2,256,256]{3,2,1,0:T(8,128)}) conditional(s32[]{:T(128)} %convert_element_type.120, () %tuple.53, (s32[]{:T(128)}, f32[4]{0:T(128)S(1)}, f32[1,256]{1,0:T(1,128)}, f32[1,256]{1,0:T(1,128)}, f32[1,2,256,256]{3,2,1,0:T(8,128)}, /*index=5*/s32[1,256,256]{2,1,0:T(8,128)}, f32[1,2,256,256]{3,2,1,0:T(8,128)}, pred[]{:T(512)}, ...), branch_computations={%region_7.8_spmd, %region_8.9_spmd} | conditional | flops 6448287744 | bytes 52999340 | solution.py:128
  121.6 18.8 %gather_fusion.7 = f32[256]{0:T(256)S(1)} fusion(f32[256,256]{1,0:T(8,128)S(1)} %get-tuple-element.611, s32[256]{0:T(256)S(1)} %bitcast.1092), kind=kCustom, calls=%fused_computation.7 | custom fusion | bytes 4096 | tf_op jit(solution)/shard_map/cond/branch_1_fun/jit(diagonal)/gather | solution.py:62
  154.6 12.6 %collective-permute-done.3 = f32[1,2,256,256]{3,2,1,0:T(8,128)S(1)} collective-permute-done((f32[1,2,256,256]{3,2,1,0:T(8,128)}, f32[1,2,256,256]{3,2,1,0:T(8,128)S(1)}, u32[]{:S(2)}, u32[]{:S(2)}) %collective-permute-start.3) | collective-permute-done | bytes 524320 | tf_op jit(solution)/shard_map/ppermute | solution.py:15
  167.2 25.7 %conditional.11 = (f32[1,2,256,256]{3,2,1,0:T(8,128)}) conditional(s32[]{:T(128)} %convert_element_type.121, () %tuple.55, (s32[]{:T(128)}, f32[4]{0:T(128)S(1)}, f32[1,256]{1,0:T(1,128)}, f32[1,256]{1,0:T(1,128)}, f32[1,2,256,256]{3,2,1,0:T(8,128)}, /*index=5*/s32[1,256,256]{2,1,0:T(8,128)}, f32[1,2,256,256]{3,2,1,0:T(8,128)}, pred[]{:T(512)}, ...), branch_computations={%region_9.10_spmd, %region_10.11_spmd} | conditional | flops 6448287744 | bytes 52999340 | solution.py:128
  197.4 2.4 fusion.235
  199.7 2.4 fusion.234
  202.1 3.9 %collective-permute-done.4 = f32[1,2,256,256]{3,2,1,0:T(8,128)} collective-permute-done((f32[1,2,256,256]{3,2,1,0:T(8,128)}, f32[1,2,256,256]{3,2,1,0:T(8,128)}, u32[]{:S(2)}, u32[]{:S(2)}) %collective-permute-start.4) | collective-permute-done | bytes 524320 | tf_op jit(solution)/shard_map/ppermute | solution.py:15
  206.0 22.9 %conditional.12 = (f32[1,2,256,256]{3,2,1,0:T(8,128)}) conditional(s32[]{:T(128)} %convert_element_type.122, () %tuple.57, (s32[]{:T(128)}, f32[4]{0:T(128)S(1)}, f32[1,256]{1,0:T(1,128)S(1)}, f32[1,256]{1,0:T(1,128)S(1)}, f32[1,2,256,256]{3,2,1,0:T(8,128)S(1)}, /*index=5*/s32[1,256,256]{2,1,0:T(8,128)S(1)}, f32[1,2,256,256]{3,2,1,0:T(8,128)S(1)}, ...), branch_computations={%region_11.12_spmd, %region_12.13_spmd} | conditional | flops 6448287744 | bytes 48796736 | solution.py:128
  213.4 2.5 gather_fusion.11
  230.3 2.5 fusion.233
  232.8 2.5 fusion.232
  235.4 2.5 fusion.231
  237.9 3.2 collective-permute-done.5
  241.1 21.5 %conditional.13 = (f32[1,2,256,256]{3,1,0,2:T(2,128)S(1)}) conditional(s32[]{:T(128)} %convert_element_type.123, () %tuple.59, (s32[]{:T(128)}, f32[4]{0:T(128)S(1)}, f32[1,256]{1,0:T(1,128)S(1)}, f32[1,256]{1,0:T(1,128)S(1)}, f32[1,2,256,256]{3,2,1,0:T(8,128)S(1)}, /*index=5*/s32[1,256,256]{2,1,0:T(8,128)S(1)}, f32[1,2,256,256]{3,2,1,0:T(8,128)S(1)}, ...), branch_computations={%region_13.14_spmd, %region_14.15_spmd} | conditional | flops 6448287744 | bytes 49845312 | solution.py:128
  247.3 2.6 gather_fusion.13
  264.7 8.6 %all-to-all-start = ((f32[4,2,256,256]{3,1,0,2:T(2,128)}), f32[4,2,256,256]{3,1,0,2:T(2,128)S(1)}, u32[]{:S(2)}, u32[]{:S(2)}) async-start(f32[4,2,256,256]{3,1,0,2:T(2,128)} %select_dynamic-update-slice_fusion), calls=%async_computation | async-start | bytes 4194304 | tf_op jit(solution)/shard_map/all_to_all | solution.py:139
  273.6 26.0 %all-to-all-done = f32[4,2,256,256]{3,1,0,2:T(2,128)S(1)} async-done(((f32[4,2,256,256]{3,1,0,2:T(2,128)}), f32[4,2,256,256]{3,1,0,2:T(2,128)S(1)}, u32[]{:S(2)}, u32[]{:S(2)}) %all-to-all-start) | async-done | bytes 2097184 | tf_op jit(solution)/shard_map/all_to_all | solution.py:139
  306.6 32.1 %all_to_all.33 = f32[128,2,8,256]{3,2,1,0:T(8,128)S(1)} all-to-all(f32[128,2,8,256]{3,2,1,0:T(8,128)S(1)} %copy.87), channel_id=1, replica_groups=mesh['layer'=4,'energy'=32] {'energy'}, dimensions={0} | all-to-all | bytes 4194304 | tf_op jit(solution)/shard_map/all_to_all | solution.py:142
  (270 shorter events, 107.2 us)
Async XLA Ops:
  3.8 15.6 %collective-permute-start = (f32[1,2,256,256]{3,2,1,0:T(8,128)S(1)}, f32[1,2,256,256]{3,2,1,0:T(8,128)S(1)}, u32[]{:S(2)}, u32[]{:S(2)}) collective-permute-start(f32[1,2,256,256]{3,2,1,0:T(8,128)S(1)} %get-tuple-element.662), channel_id=1, source_target_pairs={{0,32},{32,64},{64,96},{1,33},{33,65},{65,97},{2,34},{34,66},{66,9... | collective-permute-start | bytes 1572872 | tf_op jit(solution)/shard_map/ppermute | solution.py:15
  23.3 14.7 %collective-permute-start.1 = (f32[1,2,256,256]{3,2,1,0:T(8,128)S(1)}, f32[1,2,256,256]{3,2,1,0:T(8,128)S(1)}, u32[]{:S(2)}, u32[]{:S(2)}) collective-permute-start(f32[1,2,256,256]{3,2,1,0:T(8,128)S(1)} %get-tuple-element.663), channel_id=1, source_target_pairs={{0,32},{32,64},{64,96},{1,33},{33,65},{65,97},{2,34},{34,66},{66,9... | collective-permute-start | bytes 1572872 | tf_op jit(solution)/shard_map/ppermute | solution.py:15
  41.6 70.1 %collective-permute-start.2 = (f32[1,2,256,256]{3,2,1,0:T(8,128)S(1)}, f32[1,2,256,256]{3,2,1,0:T(8,128)S(1)}, u32[]{:S(2)}, u32[]{:S(2)}) collective-permute-start(f32[1,2,256,256]{3,2,1,0:T(8,128)S(1)} %get-tuple-element.664), channel_id=1, source_target_pairs={{0,32},{32,64},{64,96},{1,33},{33,65},{65,97},{2,34},{34,66},{66,9... | collective-permute-start | bytes 1572872 | tf_op jit(solution)/shard_map/ppermute | solution.py:15
  112.7 2.0 copy-start.10
  115.7 3.7 %copy-start.17 = (f32[1,256]{1,0:T(1,128)S(1)}, f32[1,256]{1,0:T(1,128)}, u32[]{:S(2)}) copy-start(f32[1,256]{1,0:T(1,128)} %get-tuple-element.229) | copy-start | bytes 3076 | tf_op jit(solution)/shard_map/cond
  115.7 4.2 %copy-start.23 = (f32[1,256]{1,0:T(1,128)S(1)}, f32[1,256]{1,0:T(1,128)}, u32[]{:S(2)}) copy-start(f32[1,256]{1,0:T(1,128)} %get-tuple-element.230) | copy-start | bytes 3076 | tf_op jit(solution)/shard_map/cond
  115.7 4.3 %copy-start.4 = (f32[1,2,256,256]{3,2,1,0:T(8,128)S(1)}, f32[1,2,256,256]{3,2,1,0:T(8,128)}, u32[]{:S(2)}) copy-start(f32[1,2,256,256]{3,2,1,0:T(8,128)} %get-tuple-element.535) | copy-start | bytes 1572868 | tf_op jit(solution)/shard_map/cond
  153.3 13.9 %collective-permute-start.3 = (f32[1,2,256,256]{3,2,1,0:T(8,128)}, f32[1,2,256,256]{3,2,1,0:T(8,128)S(1)}, u32[]{:S(2)}, u32[]{:S(2)}) collective-permute-start(f32[1,2,256,256]{3,2,1,0:T(8,128)} %get-tuple-element.665), channel_id=1, source_target_pairs={{0,32},{32,64},{64,96},{1,33},{33,65},{65,97},{2,34},{34,66},{66,9... | collective-permute-start | bytes 1572872 | tf_op jit(solution)/shard_map/ppermute | solution.py:15
  168.2 2.0 copy-start.11
  171.2 3.7 %copy-start.18 = (f32[1,256]{1,0:T(1,128)S(1)}, f32[1,256]{1,0:T(1,128)}, u32[]{:S(2)}) copy-start(f32[1,256]{1,0:T(1,128)} %get-tuple-element.240) | copy-start | bytes 3076 | tf_op jit(solution)/shard_map/cond
  171.2 4.4 %copy-start.24 = (f32[1,256]{1,0:T(1,128)S(1)}, f32[1,256]{1,0:T(1,128)}, u32[]{:S(2)}) copy-start(f32[1,256]{1,0:T(1,128)} %get-tuple-element.241) | copy-start | bytes 3076 | tf_op jit(solution)/shard_map/cond
  171.2 4.4 %copy-start.5 = (f32[1,2,256,256]{3,2,1,0:T(8,128)S(1)}, f32[1,2,256,256]{3,2,1,0:T(8,128)}, u32[]{:S(2)}) copy-start(f32[1,2,256,256]{3,2,1,0:T(8,128)} %get-tuple-element.546) | copy-start | bytes 1572868 | tf_op jit(solution)/shard_map/cond
  192.9 13.1 %collective-permute-start.4 = (f32[1,2,256,256]{3,2,1,0:T(8,128)}, f32[1,2,256,256]{3,2,1,0:T(8,128)}, u32[]{:S(2)}, u32[]{:S(2)}) collective-permute-start(f32[1,2,256,256]{3,2,1,0:T(8,128)} %get-tuple-element.666), channel_id=1, source_target_pairs={{0,32},{32,64},{64,96},{1,33},{33,65},{65,97},{2,34},{34,66},{66,9... | collective-permute-start | bytes 1572872 | tf_op jit(solution)/shard_map/ppermute | solution.py:15
  196.1 10.0 %copy-start = (f32[1,2,256,256]{3,2,1,0:T(8,128)S(1)}, f32[1,2,256,256]{3,2,1,0:T(8,128)}, u32[]{:S(2)}) copy-start(f32[1,2,256,256]{3,2,1,0:T(8,128)} %param.24) | copy-start | bytes 1572868
  196.1 10.0 %copy-start.6 = (f32[1,2,256,256]{3,2,1,0:T(8,128)S(1)}, f32[1,2,256,256]{3,2,1,0:T(8,128)}, u32[]{:S(2)}) copy-start(f32[1,2,256,256]{3,2,1,0:T(8,128)} %param.25) | copy-start | bytes 1572868
  196.1 10.0 %copy-start.12 = (s32[1,256,256]{2,1,0:T(8,128)S(1)}, s32[1,256,256]{2,1,0:T(8,128)}, u32[]{:S(2)}) copy-start(s32[1,256,256]{2,1,0:T(8,128)} %param.26) | copy-start | bytes 786436
  196.1 10.0 %copy-start.13 = (f32[1,256]{1,0:T(1,128)S(1)}, f32[1,256]{1,0:T(1,128)}, u32[]{:S(2)}) copy-start(f32[1,256]{1,0:T(1,128)} %param.22) | copy-start | bytes 3076
  196.1 10.0 %copy-start.19 = (f32[1,256]{1,0:T(1,128)S(1)}, f32[1,256]{1,0:T(1,128)}, u32[]{:S(2)}) copy-start(f32[1,256]{1,0:T(1,128)} %param.23) | copy-start | bytes 3076
  229.0 12.1 %collective-permute-start.5 = (f32[1,2,256,256]{3,2,1,0:T(8,128)}, f32[1,2,256,256]{3,2,1,0:T(8,128)S(1)}, u32[]{:S(2)}, u32[]{:S(2)}) collective-permute-start(f32[1,2,256,256]{3,2,1,0:T(8,128)} %get-tuple-element.667), channel_id=1, source_target_pairs={{0,32},{32,64},{64,96},{1,33},{33,65},{65,97},{2,34},{34,66},{66,9... | collective-permute-start | bytes 1572872 | tf_op jit(solution)/shard_map/ppermute | solution.py:15
  264.7 8.6 %copy-start.26 = (s32[8]{0:T(128)S(1)}, s32[8]{0:T(128)}, u32[]{:S(2)}) copy-start(s32[8]{0:T(128)} %param.29) | copy-start | bytes 100
  264.7 8.7 %copy-start.25 = (f32[8]{0:T(128)S(1)}, f32[8]{0:T(128)}, u32[]{:S(2)}) copy-start(f32[8]{0:T(128)} %param.28) | copy-start | bytes 100
  264.7 34.9 %all-to-all-start = ((f32[4,2,256,256]{3,1,0,2:T(2,128)}), f32[4,2,256,256]{3,1,0,2:T(2,128)S(1)}, u32[]{:S(2)}, u32[]{:S(2)}) async-start(f32[4,2,256,256]{3,1,0,2:T(2,128)} %select_dynamic-update-slice_fusion), calls=%async_computation | async-start | bytes 4194304 | tf_op jit(solution)/shard_map/all_to_all | solution.py:139
where the time goes:
time: 347 us; the launch traced here: 341 us
  waiting for transfers between devices  142 us (41%)
  matrix products  53.8 us (16%)
  local copies, waits for them, and re-layouts  48 us (14%)
  other arithmetic  33.8 us (10%)
  blocking collectives  32.1 us (9%)
  starting transfers between devices  16.3 us (5%)
  loops' own time  13.7 us (4%)
    ppermute x6, waiting for transfers between devices, from_behind(): return lax.ppermute(block, axis, route)  116 us
    dot_general x128, matrix products, matmul_high(): return jnp.matmul(first_op, second_op, precision=exact_mode)  51.9 us
    all_to_all x1, blocking collectives, local(): lax.all_to_all(blended, 'energy', split_axis=0, concat_axis=2, tiled=True)  32.1 us
    gather x4, local copies, waits for them, and re-layouts, solve_layer(): diag_imag = jnp.diagonal(system[:, 1], axis1=-2, axis2=-1)  26.3 us
    all_to_all x1, waiting for transfers between devices, local(): lax.all_to_all(green_blocks, 'energy', split_axis=2, concat_axis=0, tiled...  26 us
    dynamic_update_slice x7, other arithmetic, local(): lax.dynamic_update_slice_in_dim(green_blocks, jnp.where(active, result_bl...  15.7 us
    another operation x7, loops' own time, local(): result_block = lax.cond(active, advance, resting, (offset_row, entering))  13.7 us
    gather x4, local copies, waits for them, and re-layouts, solve_layer(): diag_real = jnp.diagonal(system[:, 0], axis1=-2, axis2=-1)  9.37 us
  transfers between devices with their start and end apart: 7, of which 7 were waited for; matrix products, arithmetic and copies ran while one was open for 5% of the time, Pallas kernels for 0%

commit v1 on v0

v1 whole, which is shorter than its diff:
```python
import functools

import jax
import jax.numpy as jnp
from jax import lax
from jax.experimental import pallas as pl
from jax.experimental.pallas import tpu as pltpu
from jax.sharding import PartitionSpec as P

MESH = pl.DeviceIdType.MESH
F32 = jnp.float32
BF16 = jnp.bfloat16
OWN = 4
SLOTS = 18
TAPS = 8


def split(value):
    high = value.astype(BF16)
    low = (value - high.astype(F32)).astype(BF16)
    return high, low


def dot(a, b):
    return jnp.dot(a, b, preferred_element_type=F32)


def product(first, second):
    fh, fl = first
    sh, sl = second
    n = sh.shape[0] // 2

    def against(part):
        rows = slice(part * n, (part + 1) * n)
        return dot(fh, sh[rows]) + (dot(fl, sh[rows]) + dot(fh, sl[rows]))

    real, imag = against(0), against(1)
    return real[:n] - imag[n:], real[n:] + imag[:n]


def kernel(
    layers,
    groups,
    onsite,
    broad,
    weights,
    offsets,
    ham,
    coup,
    mask,
    prior,
    out,
    prior_v,
    ham_v,
    coup_v,
    mask_v,
    slots,
    inc,
    acc,
    base,
    c_h,
    c_l,
    ch_h,
    ch_l,
    table,
    load_sem,
    prior_sem,
    xs_sem,
    xr_sem,
    near_sem,
    far_sem,
    skip_sem,
    fwd_sem,
    slot_sem,
    out_sem,
    token,
):
    n = onsite.shape[-1]
    x = lax.axis_index("layer")
    m = lax.axis_index("energy")
    odd = lax.rem(m, 2)
    sign = 1 - 2 * odd
    near = m + sign
    far = m - sign
    skip = m + 2 * sign
    behind = m - 2 * sign
    near_ok = jnp.logical_and(skip >= 0, skip < groups)
    far_ok = jnp.logical_and(far >= 0, far < groups)
    first_layer = x == 0
    has_next = x < layers - 1

    def place(t):
        return jnp.where(odd == 1, OWN - 1 - t, t)

    loads = [
        pltpu.make_async_copy(coup, coup_v, load_sem.at[0]),
        pltpu.make_async_copy(mask, mask_v, load_sem.at[1]),
        pltpu.make_async_copy(ham, ham_v, load_sem.at[2]),
    ]
    for load in loads:
        load.start()

    def prior_load(t):
        return pltpu.make_async_copy(prior.at[place(t)], prior_v.at[t], prior_sem.at[t])

    for t in range(OWN):
        prior_load(t).start()

    barrier = pltpu.get_barrier_semaphore()
    pl.semaphore_signal(barrier, inc=1, device_id=(x, near), device_id_type=MESH)

    @pl.when(far_ok)
    def _():
        pl.semaphore_signal(barrier, inc=1, device_id=(x, far), device_id_type=MESH)
        pl.semaphore_signal(barrier, inc=1, device_id=(x, behind), device_id_type=MESH)

    @pl.when(x > 0)
    def _():
        pl.semaphore_signal(barrier, inc=1, device_id=(x - 1, m), device_id_type=MESH)

    for i in range(SLOTS + 3):
        tap = F32(0.0)
        for j in range(TAPS):
            tap = tap + jnp.where(offsets[j] * sign == i - 10, weights[j], F32(0.0))
        table[i] = tap

    acc[...] = jnp.zeros_like(acc)

    @pl.when(jnp.logical_not(far_ok))
    def _():
        slots[0:7] = jnp.zeros((7, 2 * n, n), F32)

    @pl.when(jnp.logical_not(near_ok))
    def _():
        slots[15:18] = jnp.zeros((3, 2 * n, n), F32)

    loads[0].wait()
    loads[1].wait()
    kept = mask_v[...].astype(F32)
    c_real, c_imag = coup_v[:n] * kept, coup_v[n:] * kept
    for half, part in ((0, c_real), (1, c_imag)):
        c_h[half * n : (half + 1) * n], c_l[half * n : (half + 1) * n] = split(part)
    for half, part in ((0, c_real.T), (1, -c_imag.T)):
        ch_h[half * n : (half + 1) * n], ch_l[half * n : (half + 1) * n] = split(part)
    loads[2].wait()
    base[:n] = 0.5 * (ham_v[:n] + ham_v[:n].T)
    base[n:] = 0.5 * (ham_v[n:] - ham_v[n:].T)

    @pl.when(first_layer)
    def _():
        into = jnp.concatenate([0.5 * (coup_v[n:] * mask_v[...].astype(F32)), -0.5 * (coup_v[:n] * mask_v[...].astype(F32))])
        real, imag = product(split(into), (ch_h[...], ch_l[...]))
        base[:n] += real
        base[n:] += imag

    pl.semaphore_wait(
        barrier,
        1 + far_ok.astype(jnp.int32) + near_ok.astype(jnp.int32) + has_next.astype(jnp.int32),
    )

    rows_first = 3 * n // 2

    def to_next(t, part):
        rows = pl.ds(0, rows_first) if part == 0 else pl.ds(rows_first, 2 * n - rows_first)
        return pltpu.make_async_remote_copy(
            src_ref=slots.at[7 + t, rows],
            dst_ref=inc.at[t, rows],
            send_sem=xs_sem.at[t, part],
            recv_sem=xr_sem.at[t, part],
            device_id=(jnp.minimum(x + 1, layers - 1), m),
            device_id_type=MESH,
        )

    def send(source, target, send_sem, device):
        return pltpu.make_async_remote_copy(
            src_ref=slots.at[source],
            dst_ref=slots.at[target],
            send_sem=send_sem,
            recv_sem=slot_sem.at[target],
            device_id=(x, device),
            device_id_type=MESH,
        )

    def to_near(t):
        return send(7 + t, 14 - t, near_sem.at[t], near)

    def to_far(t):
        return send(7 + t, 6 - t, far_sem.at[t], far)

    def to_skip(t):
        return send(7 + t, t - 1, skip_sem.at[t], skip)

    def forward(t):
        return send(6 - t, 15 + t, fwd_sem.at[t], near)

    def arrived(slot):
        send(slot, slot, near_sem.at[0], near).wait_recv()

    def accumulate(sources):
        taps = [[table[u - v + 3] for v in range(OWN)] for u in sources]

        def body(c, carry):
            rows = pl.ds(pl.multiple_of(c * 16, 16), 16)
            blocks = [slots[u, rows, :] for u in sources]
            for v in range(OWN):
                total = acc[v, rows, :]
                for s in range(len(sources)):
                    total = total + taps[s][v] * blocks[s]
                acc[v, rows, :] = total
            return carry

        lax.fori_loop(0, 2 * n // 16, body, 0)

    def gather(t):
        @pl.when(far_ok)
        def _():
            arrived(6 - t)

            @pl.when(t < OWN - 1)
            def _():
                forward(t).start()

        arrived(14 - t)
        accumulate([7 + t, 14 - t, 6 - t])

        @pl.when(t > 0)
        def _():
            @pl.when(far_ok)
            def _():
                arrived(t - 1)

            @pl.when(near_ok)
            def _():
                arrived(14 + t)

            accumulate([t - 1, 14 + t])

    eye = lax.broadcasted_iota(jnp.int32, (n, n), 0) == lax.broadcasted_iota(jnp.int32, (n, n), 1)

    def step(t, carry):
        prior_load(t).wait()
        contact = slots.at[7 + t]

        @pl.when(first_layer)
        def _():
            contact[...] = base[...] + prior_v[t]

        @pl.when(jnp.logical_not(first_layer))
        def _():
            to_next(t, 0).wait_recv()
            to_next(t, 1).wait_recv()
            half_way = jnp.concatenate(product((c_h[...], c_l[...]), split(inc[t])))
            real, imag = product(split(half_way), (ch_h[...], ch_l[...]))
            contact[:n] = real + (base[:n] + prior_v[t, :n])
            contact[n:] = imag + (base[n:] + prior_v[t, n:])

        energy = (m * OWN + place(t)).astype(F32)
        level = -1.0 + 2.0 * (energy + 0.5) / (groups * OWN)
        real, imag = contact[:n], contact[n:]
        diag_real = (level - onsite[...]) - jnp.sum(jnp.where(eye, real, 0.0), axis=0, keepdims=True)
        diag_imag = broad[...] - jnp.sum(jnp.where(eye, imag, 0.0), axis=0, keepdims=True)
        modulus = diag_real * diag_real + diag_imag * diag_imag
        inv_real, inv_imag = diag_real / modulus, -diag_imag / modulus
        col_real = jnp.sum(jnp.where(eye, inv_real, 0.0), axis=1, keepdims=True)
        col_imag = jnp.sum(jnp.where(eye, inv_imag, 0.0), axis=1, keepdims=True)
        real, imag = jnp.where(eye, 0.0, real), jnp.where(eye, 0.0, imag)
        res_real = real * inv_real - imag * inv_imag
        res_imag = real * inv_imag + imag * inv_real
        one_real = jnp.where(eye, inv_real, col_real * res_real - col_imag * res_imag)
        one_imag = jnp.where(eye, inv_imag, col_real * res_imag + col_imag * res_real)
        residue = split(jnp.concatenate([res_real, res_imag]))
        square = jnp.concatenate(product(residue, residue))
        square = split(square)
        one = jnp.concatenate([one_real, one_imag])
        fourth = split(jnp.concatenate(product(square, square)))
        real, imag = product(split(one), square)
        two = one + jnp.concatenate([real, imag])
        real, imag = product(split(two), fourth)
        slots[7 + t] = two + jnp.concatenate([real, imag])

        @pl.when(far_ok)
        def _():
            to_far(t).start()

        @pl.when(jnp.logical_and(near_ok, t > 0))
        def _():
            to_skip(t).start()

        @pl.when(has_next)
        def _():
            @pl.when(jnp.logical_and(first_layer, t + odd > 0))
            def _():
                pl.semaphore_wait(token, 1)

            to_next(t, 0).start()
            to_next(t, 1).start()

        to_near(t).start()

        @pl.when(t > 0)
        def _():
            gather(t - 1)

        @pl.when(first_layer)
        def _():
            to_next(t, 0).wait_send()

            @pl.when(jnp.logical_or(odd == 0, t < OWN - 1))
            def _():
                pl.semaphore_signal(token, inc=1, device_id=(x, near), device_id_type=MESH)

        return carry

    lax.fori_loop(0, OWN, step, 0)
    gather(OWN - 1)

    stores = [
        pltpu.make_async_copy(acc.at[v], out.at[place(v)], out_sem.at[v]) for v in range(OWN)
    ]
    for store in stores:
        store.start()

    for t in range(OWN):
        to_near(t).wait_send()

        @pl.when(has_next)
        def _():
            @pl.when(jnp.logical_not(first_layer))
            def _():
                to_next(t, 0).wait_send()

            to_next(t, 1).wait_send()

        @pl.when(far_ok)
        def _():
            to_far(t).wait_send()
            if t < OWN - 1:
                forward(t).wait_send()

        if t > 0:

            @pl.when(near_ok)
            def _():
                to_skip(t).wait_send()

    for store in stores:
        store.wait()


def solution(mesh):
    layers, groups = mesh.shape["layer"], mesh.shape["energy"]

    def local(onsite, broad, ham, coup, mask, prior, weights, offsets):
        n = onsite.shape[-1]
        hbm = pl.BlockSpec(memory_space=pl.ANY)
        vmem = pl.BlockSpec(memory_space=pltpu.VMEM)
        smem = pl.BlockSpec(memory_space=pltpu.SMEM)
        block = (2 * n, n)
        result = pl.pallas_call(
            functools.partial(kernel, layers, groups),
            out_shape=jax.ShapeDtypeStruct((OWN, 2 * n, n), F32),
            in_specs=[vmem, vmem, smem, smem, hbm, hbm, hbm, hbm],
            out_specs=hbm,
            scratch_shapes=[
                pltpu.VMEM((OWN, *block), F32),
                pltpu.VMEM(block, F32),
                pltpu.VMEM(block, F32),
                pltpu.VMEM((n, n), jnp.int32),
                pltpu.VMEM((SLOTS, *block), F32),
                pltpu.VMEM((OWN, *block), F32),
                pltpu.VMEM((OWN, *block), F32),
                pltpu.VMEM(block, F32),
                pltpu.VMEM(block, BF16),
                pltpu.VMEM(block, BF16),
                pltpu.VMEM(block, BF16),
                pltpu.VMEM(block, BF16),
                pltpu.SMEM((SLOTS + 3,), F32),
                pltpu.SemaphoreType.DMA((3,)),
                pltpu.SemaphoreType.DMA((OWN,)),
                pltpu.SemaphoreType.DMA((OWN, 2)),
                pltpu.SemaphoreType.DMA((OWN, 2)),
                pltpu.SemaphoreType.DMA((OWN,)),
                pltpu.SemaphoreType.DMA((OWN,)),
                pltpu.SemaphoreType.DMA((OWN,)),
                pltpu.SemaphoreType.DMA((OWN,)),
                pltpu.SemaphoreType.DMA((SLOTS,)),
                pltpu.SemaphoreType.DMA((OWN,)),
                pltpu.SemaphoreType.REGULAR,
            ],
            compiler_params=pltpu.CompilerParams(
                collective_id=0, has_side_effects=True, vmem_limit_bytes=50 * 2**20
            ),
        )(
            onsite,
            broad,
            weights,
            offsets,
            ham.reshape(block),
            coup.reshape(block),
            mask.reshape(n, n),
            prior.reshape(OWN, *block),
        )
        return result.reshape(1, OWN, 2, n, n)

    return jax.shard_map(
        local,
        mesh=mesh,
        in_specs=(
            P("layer", None),
            P("layer", None),
            P("layer", None, None, None),
            P("layer", None, None, None),
            P("layer", None, None),
            P("layer", "energy", None, None, None),
            P(),
            P(),
        ),
        out_specs=P("layer", "energy", None, None, None),
        check_vma=False,
    )
```

time: 347 us -> 106 us (0.31); the launches traced: 341 us -> 105 us
  waiting for transfers between devices: 142 us -> 0 us
  Pallas kernels: 0 us -> 98.4 us
  matrix products: 53.8 us -> 0 us
  local copies, waits for them, and re-layouts: 48 us -> 7.02 us
  other arithmetic: 33.8 us -> 0 us
  blocking collectives: 32.1 us -> 0 us
  starting transfers between devices: 16.3 us -> 0 us
  loops' own time: 13.7 us -> 0 us
    ppermute x6 -> x0, waiting for transfers between devices: 116 us -> none  [from_behind(): return lax.ppermute(block, axis, route)]
    pallas_call x0 -> x1, Pallas kernels: none -> 98.4 us  [local(): pl.pallas_call(functools.partial(kernel, layers, groups), out_shape=jax.S...]
    dot_general x129 -> x0, matrix products: 53.8 us -> none  [the longest x128 51.9 us: matmul_high(): return jnp.matmul(first_op, second_op, precision=exact_mode)]
    gather x8 -> x0, local copies, waits for them, and re-layouts: 35.7 us -> none  [the longest x4 26.3 us: solve_layer(): diag_imag = jnp.diagonal(system[:, 1], axis1=-2, axis2=-1)]
    all_to_all x1 -> x0, blocking collectives: 32.1 us -> none  [local(): lax.all_to_all(blended, 'energy', split_axis=0, concat_axis=2, tiled=True)]
    all_to_all x1 -> x0, waiting for transfers between devices: 26 us -> none  [local(): lax.all_to_all(green_blocks, 'energy', split_axis=2, concat_axis=0, tiled...]
    dynamic_update_slice x7 -> x0, other arithmetic: 15.7 us -> none  [local(): lax.dynamic_update_slice_in_dim(green_blocks, jnp.where(active, result_bl...]
    another operation x7 -> x0, loops' own time: 13.7 us -> none  [local(): result_block = lax.cond(active, advance, resting, (offset_row, entering))]
  transfers between devices with their start and end apart: 7 -> 0, of which waited for: 7 -> 0; matrix products, arithmetic and copies ran while one was open for 5% -> 0% of each run, Pallas kernels for 0% -> 0%
where the time goes in v1:
time: 106 us; the launch traced here: 105 us
  Pallas kernels  98.4 us (93%)
  local copies, waits for them, and re-layouts  7.02 us (7%)
    pallas_call x1, Pallas kernels, local(): pl.pallas_call(functools.partial(kernel, layers, groups), out_shape=jax.S...  98.4 us
    unnamed x15, local copies, waits for them, and re-layouts  7.02 us

profile of v1, /device:TPU:30, one launch (start us, length us, event | category | flops | bytes accessed | tf_op | source)
XLA Modules:
  0.0 105.4 jit_solution(10982951705102546237)
XLA Ops:
  0.0 0.0 copy-start
  0.0 1.0 copy-done
  1.0 0.0 copy-start.1
  1.0 1.0 copy-done.1
  2.1 0.0 copy-start.2
  2.1 0.9 copy-done.2
  3.0 0.0 copy-start.3
  3.0 0.7 copy-done.3
  3.7 0.0 copy-start.4
  3.7 0.7 copy-done.4
  4.4 0.0 copy-start.5
  4.4 0.7 copy-done.5
  5.0 0.0 copy-start.6
  5.1 0.7 copy-done.6
  5.7 98.4 %shard_map.82 = f32[4,512,256]{2,1,0:T(8,128)S(1)} custom-call(f32[1,256]{1,0:T(1,128)S(1)} %copy-done.3, f32[1,256]{1,0:T(1,128)S(1)} %copy-done.4, f32[8]{0:T(128)S(1)} %copy-done.5, s32[8]{0:T(128)S(1)} %copy-done.6, f32[512,256]{1,0:T(8,128)S(1)} %bitcast.6, f32[512,256]{1,0:T(8,128)S(1)} %bitcast.7, s32[256,256]{1,0:T(8,128)S(1)} %bitcast.8, ...), custom_call_target="tpu_custom_call" | custom-call | tf_op jit(solution)/shard_map/pallas_call | solution.py:359
  104.1 1.3 %copy.10 = f32[1,4,2,256,256]{4,3,2,1,0:T(8,128)} copy(f32[1,4,2,256,256]{4,3,2,1,0:T(8,128)S(1)} %bitcast.5) | data formatting | bytes 4194304
Async XLA Ops:
  0.0 1.0 copy-start
  1.0 1.0 copy-start.1
  2.1 0.9 copy-start.2
  3.0 0.7 copy-start.3
  3.7 0.7 copy-start.4
  4.4 0.7 copy-start.5
  5.0 0.7 copy-start.6

commit v2 on v1

v2 whole, which is shorter than its diff:
```python
import functools

import jax
import jax.numpy as jnp
from jax import lax
from jax.experimental import pallas as pl
from jax.experimental.pallas import tpu as pltpu
from jax.sharding import PartitionSpec as P

MESH = pl.DeviceIdType.MESH
F32 = jnp.float32
BF16 = jnp.bfloat16
OWN = 4
SLOTS = 18
TAPS = 8


def split(value):
    high = value.astype(BF16)
    low = (value - high.astype(F32)).astype(BF16)
    return high, low


def dot(a, b):
    return jnp.dot(a, b, preferred_element_type=F32)


def halves(first, second, n):
    fh, fl = first
    sh, sl = second
    re, im = slice(0, n), slice(n, 2 * n)

    def three(rows, part):
        return dot(fh[rows], sh[part]) + (dot(fl[rows], sh[part]) + dot(fh[rows], sl[part]))

    yield three(re, re) - three(im, im)
    yield three(im, re) + three(re, im)


def kernel(
    layers,
    groups,
    onsite,
    broad,
    weights,
    offsets,
    ham,
    coup,
    mask,
    prior,
    out,
    onsite_v,
    broad_v,
    weights_s,
    offsets_s,
    prior_v,
    ham_v,
    coup_v,
    mask_v,
    slots,
    inc,
    acc,
    base,
    contact,
    one,
    two,
    pairs,
    table,
    load_sem,
    prior_sem,
    xs_sem,
    xr_sem,
    near_sem,
    far_sem,
    skip_sem,
    fwd_sem,
    slot_sem,
    out_sem,
    token,
):
    n = onsite.shape[-1]
    x = lax.axis_index("layer")
    m = lax.axis_index("energy")
    odd = lax.rem(m, 2)
    sign = 1 - 2 * odd
    near = m + sign
    far = m - sign
    skip = m + 2 * sign
    behind = m - 2 * sign
    near_ok = jnp.logical_and(skip >= 0, skip < groups)
    far_ok = jnp.logical_and(far >= 0, far < groups)
    first_layer = x == 0
    later_layer = x > 0
    has_next = x < layers - 1
    re, im = slice(0, n), slice(n, 2 * n)
    coupled, adjoint, along, residue, square, first_sum, fourth, second_sum = (
        (pairs.at[2 * i], pairs.at[2 * i + 1]) for i in range(8)
    )

    def keep(pair, rows, value):
        pair[0][rows], pair[1][rows] = split(value)

    def place(t):
        return jnp.where(odd == 1, OWN - 1 - t, t)

    def prior_load(t):
        return pltpu.make_async_copy(prior.at[place(t)], prior_v.at[t], prior_sem.at[t])

    loads = [
        pltpu.make_async_copy(source, target, load_sem.at[i])
        for i, (source, target) in enumerate(
            [
                (coup, coup_v),
                (mask, mask_v),
                (ham, ham_v),
                (onsite, onsite_v),
                (broad, broad_v),
                (weights, weights_s),
                (offsets, offsets_s),
            ]
        )
    ]
    for load in loads[:3]:
        load.start()
    prior_load(0).start()
    for load in loads[3:]:
        load.start()
    for t in range(1, OWN):
        prior_load(t).start()

    barrier = pltpu.get_barrier_semaphore()
    pl.semaphore_signal(barrier, inc=1, device_id=(x, near), device_id_type=MESH)

    @pl.when(far_ok)
    def _():
        pl.semaphore_signal(barrier, inc=1, device_id=(x, far), device_id_type=MESH)
        pl.semaphore_signal(barrier, inc=1, device_id=(x, behind), device_id_type=MESH)

    @pl.when(later_layer)
    def _():
        pl.semaphore_signal(barrier, inc=1, device_id=(x - 1, m), device_id_type=MESH)

    def prepare():
        acc[...] = jnp.zeros_like(acc)

        @pl.when(jnp.logical_not(far_ok))
        def _():
            slots[0:7] = jnp.zeros((7, 2 * n, n), F32)

        @pl.when(jnp.logical_not(near_ok))
        def _():
            slots[15:18] = jnp.zeros((3, 2 * n, n), F32)

        loads[5].wait()
        loads[6].wait()
        for i in range(SLOTS + 3):
            tap = F32(0.0)
            for j in range(TAPS):
                tap = tap + jnp.where(offsets_s[j] * sign == i - 10, weights_s[j], F32(0.0))
            table[i] = tap

    loads[0].wait()
    loads[1].wait()
    kept = mask_v[...].astype(F32)
    coup_v[re] = coup_v[re] * kept
    coup_v[im] = coup_v[im] * kept
    keep(coupled, re, coup_v[re])
    keep(coupled, im, coup_v[im])
    keep(adjoint, re, coup_v[re].T)
    keep(adjoint, im, -coup_v[im].T)
    loads[2].wait()
    base[re] = 0.5 * (ham_v[re] + ham_v[re].T)
    base[im] = 0.5 * (ham_v[im] - ham_v[im].T)
    loads[3].wait()
    loads[4].wait()

    @pl.when(first_layer)
    def _():
        keep(along, re, 0.5 * coup_v[im])
        keep(along, im, -0.5 * coup_v[re])
        for rows, part in zip((re, im), halves(along, adjoint, n)):
            base[rows] += part

    @pl.when(later_layer)
    def _():
        prepare()

    pl.semaphore_wait(
        barrier,
        1 + far_ok.astype(jnp.int32) + near_ok.astype(jnp.int32) + has_next.astype(jnp.int32),
    )

    quarter = n // 2

    def to_next(t, part):
        rows = pl.ds(part * quarter, quarter)
        return pltpu.make_async_remote_copy(
            src_ref=slots.at[7 + t, rows],
            dst_ref=inc.at[t, rows],
            send_sem=xs_sem.at[t, part],
            recv_sem=xr_sem.at[t, part],
            device_id=(jnp.minimum(x + 1, layers - 1), m),
            device_id_type=MESH,
        )

    def send(source, target, send_sem, device):
        return pltpu.make_async_remote_copy(
            src_ref=slots.at[source],
            dst_ref=slots.at[target],
            send_sem=send_sem,
            recv_sem=slot_sem.at[target],
            device_id=(x, device),
            device_id_type=MESH,
        )

    def to_near(t):
        return send(7 + t, 14 - t, near_sem.at[t], near)

    def to_far(t):
        return send(7 + t, 6 - t, far_sem.at[t], far)

    def to_skip(t):
        return send(7 + t, t - 1, skip_sem.at[t], skip)

    def forward(t):
        return send(6 - t, 15 + t, fwd_sem.at[t], near)

    def arrived(slot):
        send(slot, slot, near_sem.at[0], near).wait_recv()

    def accumulate(sources):
        taps = [[table[u - v + 3] for v in range(OWN)] for u in sources]

        def body(c, carry):
            rows = pl.ds(pl.multiple_of(c * 16, 16), 16)
            blocks = [slots[u, rows, :] for u in sources]
            for v in range(OWN):
                total = acc[v, rows, :]
                for s in range(len(sources)):
                    total = total + taps[s][v] * blocks[s]
                acc[v, rows, :] = total
            return carry

        lax.fori_loop(0, 2 * n // 16, body, 0)

    def gather(t):
        @pl.when(far_ok)
        def _():
            arrived(6 - t)

            @pl.when(t < OWN - 1)
            def _():
                forward(t).start()

        arrived(14 - t)
        accumulate([7 + t, 14 - t, 6 - t])

        @pl.when(t > 0)
        def _():
            @pl.when(far_ok)
            def _():
                arrived(t - 1)

            @pl.when(near_ok)
            def _():
                arrived(14 + t)

            accumulate([t - 1, 14 + t])

    eye = lax.broadcasted_iota(jnp.int32, (n, n), 0) == lax.broadcasted_iota(jnp.int32, (n, n), 1)

    def reciprocal(diag_real, diag_imag):
        modulus = diag_real * diag_real + diag_imag * diag_imag
        columns = diag_real / modulus, -diag_imag / modulus
        return [
            (column, jnp.sum(jnp.where(eye, column, 0.0), axis=0, keepdims=True))
            for column in columns
        ]

    def start_sweeps(q, size, real, imag, inverse):
        rows = slice(q * size, (q + 1) * size)
        (col_real, row_real), (col_imag, row_imag) = inverse
        on = eye[rows]
        real, imag = jnp.where(on, 0.0, real), jnp.where(on, 0.0, imag)
        res_real = real * row_real - imag * row_imag
        res_imag = real * row_imag + imag * row_real
        keep(residue, rows, res_real)
        keep(residue, slice(n + q * size, n + (q + 1) * size), res_imag)
        cr, ci = col_real[rows], col_imag[rows]
        one[q * size : (q + 1) * size] = jnp.where(on, row_real, cr * res_real - ci * res_imag)
        one[n + q * size : n + (q + 1) * size] = jnp.where(on, row_imag, cr * res_imag + ci * res_real)

    def step(t, carry):
        prior_load(t).wait()
        energy = (m * OWN + place(t)).astype(F32)
        level = -1.0 + 2.0 * (energy + 0.5) / (groups * OWN)
        contact[...] = base[...] + prior_v[t]
        diag_real = jnp.sum(jnp.where(eye, (level - onsite_v[...]) - contact[re], 0.0), axis=1, keepdims=True)
        diag_imag = jnp.sum(jnp.where(eye, broad_v[...] - contact[im], 0.0), axis=1, keepdims=True)

        @pl.when(first_layer)
        def _():
            start_sweeps(0, n, contact[re], contact[im], reciprocal(diag_real, diag_imag))

        @pl.when(later_layer)
        def _():
            to_next(t, 0).wait_recv()
            to_next(t, 1).wait_recv()
            (ch, cl), (in_h, in_l) = coupled, fourth
            keep(fourth, re, inc[t, re])
            left = dot(ch[...], in_h[re]) + (dot(cl[...], in_h[re]) + dot(ch[...], in_l[re]))
            to_next(t, 2).wait_recv()
            to_next(t, 3).wait_recv()
            keep(fourth, im, inc[t, im])
            right = dot(ch[...], in_h[im]) + (dot(cl[...], in_h[im]) + dot(ch[...], in_l[im]))
            way_real, way_imag = left[re] - right[im], left[im] + right[re]
            keep(along, re, way_real)
            keep(along, im, way_imag)
            c_real, c_imag = coup_v[re], coup_v[im]
            inverse = reciprocal(
                diag_real - jnp.sum(way_real * c_real + way_imag * c_imag, axis=1, keepdims=True),
                diag_imag - jnp.sum(way_imag * c_real - way_real * c_imag, axis=1, keepdims=True),
            )
            size = n // 2
            (ah, al), (dh, dl) = along, adjoint
            for q in range(2):
                top, low = slice(q * size, (q + 1) * size), slice(n + q * size, n + (q + 1) * size)

                def three(rows, part):
                    return dot(ah[rows], dh[part]) + (dot(al[rows], dh[part]) + dot(ah[rows], dl[part]))

                real = three(top, re) - three(low, im) + contact[top]
                imag = three(low, re) + three(top, im) + contact[low]
                start_sweeps(q, size, real, imag, inverse)

        for rows, part in zip((re, im), halves(residue, residue, n)):
            keep(square, rows, part)
        for rows in (re, im):
            keep(first_sum, rows, one[rows])
        for rows, part in zip((re, im), halves(first_sum, square, n)):
            two[rows] = one[rows] + part
            keep(second_sum, rows, two[rows])
        for rows, part in zip((re, im), halves(square, square, n)):
            keep(fourth, rows, part)
        at_once = jnp.logical_and(has_next, jnp.logical_or(later_layer, t + odd == 0))
        for parts, rows, part in zip(((0, 1), (2, 3)), (re, im), halves(second_sum, fourth, n)):
            slots[7 + t, rows] = two[rows] + part

            @pl.when(at_once)
            def _():
                for p in parts:
                    to_next(t, p).start()

        @pl.when(far_ok)
        def _():
            to_far(t).start()

        @pl.when(jnp.logical_and(near_ok, t > 0))
        def _():
            to_skip(t).start()

        to_near(t).start()

        @pl.when(jnp.logical_and(first_layer, t + odd > 0))
        def _():
            pl.semaphore_wait(token, 1)
            for p in range(4):
                to_next(t, p).start()

        @pl.when(jnp.logical_and(first_layer, t == 0))
        def _():
            prepare()

        @pl.when(t > 0)
        def _():
            gather(t - 1)

        @pl.when(first_layer)
        def _():
            for p in range(3):
                to_next(t, p).wait_send()

            @pl.when(jnp.logical_or(odd == 0, t < OWN - 1))
            def _():
                pl.semaphore_signal(token, inc=1, device_id=(x, near), device_id_type=MESH)

        return carry

    lax.fori_loop(0, OWN, step, 0)
    gather(OWN - 1)

    stores = [
        pltpu.make_async_copy(acc.at[v], out.at[place(v)], out_sem.at[v]) for v in range(OWN)
    ]
    for store in stores:
        store.start()

    for t in range(OWN):
        to_near(t).wait_send()

        @pl.when(has_next)
        def _():
            @pl.when(later_layer)
            def _():
                for p in range(3):
                    to_next(t, p).wait_send()

            to_next(t, 3).wait_send()

        @pl.when(far_ok)
        def _():
            to_far(t).wait_send()
            if t < OWN - 1:
                forward(t).wait_send()

        if t > 0:

            @pl.when(near_ok)
            def _():
                to_skip(t).wait_send()

    for store in stores:
        store.wait()


def solution(mesh):
    layers, groups = mesh.shape["layer"], mesh.shape["energy"]

    def local(onsite, broad, ham, coup, mask, prior, weights, offsets):
        n = onsite.shape[-1]
        hbm = pl.BlockSpec(memory_space=pltpu.HBM)
        block = (2 * n, n)
        result = pl.pallas_call(
            functools.partial(kernel, layers, groups),
            out_shape=jax.ShapeDtypeStruct((OWN, 2 * n, n), F32),
            in_specs=[hbm] * 8,
            out_specs=hbm,
            scratch_shapes=[
                pltpu.VMEM((1, n), F32),
                pltpu.VMEM((1, n), F32),
                pltpu.SMEM((TAPS,), F32),
                pltpu.SMEM((TAPS,), jnp.int32),
                pltpu.VMEM((OWN, *block), F32),
                pltpu.VMEM(block, F32),
                pltpu.VMEM(block, F32),
                pltpu.VMEM((n, n), jnp.int32),
                pltpu.VMEM((SLOTS, *block), F32),
                pltpu.VMEM((OWN, *block), F32),
                pltpu.VMEM((OWN, *block), F32),
                pltpu.VMEM(block, F32),
                pltpu.VMEM(block, F32),
                pltpu.VMEM(block, F32),
                pltpu.VMEM(block, F32),
                pltpu.VMEM((16, *block), BF16),
                pltpu.SMEM((SLOTS + 3,), F32),
                pltpu.SemaphoreType.DMA((7,)),
                pltpu.SemaphoreType.DMA((OWN,)),
                pltpu.SemaphoreType.DMA((OWN, 4)),
                pltpu.SemaphoreType.DMA((OWN, 4)),
                pltpu.SemaphoreType.DMA((OWN,)),
                pltpu.SemaphoreType.DMA((OWN,)),
                pltpu.SemaphoreType.DMA((OWN,)),
                pltpu.SemaphoreType.DMA((OWN,)),
                pltpu.SemaphoreType.DMA((SLOTS,)),
                pltpu.SemaphoreType.DMA((OWN,)),
                pltpu.SemaphoreType.REGULAR,
            ],
            compiler_params=pltpu.CompilerParams(
                collective_id=0, has_side_effects=True, vmem_limit_bytes=62 * 2**20
            ),
        )(
            onsite,
            broad,
            weights,
            offsets,
            ham.reshape(block),
            coup.reshape(block),
            mask.reshape(n, n),
            prior.reshape(OWN, *block),
        )
        return result.reshape(1, OWN, 2, n, n)

    return jax.shard_map(
        local,
        mesh=mesh,
        in_specs=(
            P("layer", None),
            P("layer", None),
            P("layer", None, None, None),
            P("layer", None, None, None),
            P("layer", None, None),
            P("layer", "energy", None, None, None),
            P(),
            P(),
        ),
        out_specs=P("layer", "energy", None, None, None),
        check_vma=False,
    )
```

time: 106 us -> 99.4 us (0.938)
  local copies, waits for them, and re-layouts: 7.02 us -> 3.05 us
  Pallas kernels: 98.4 us -> 96.2 us
    unnamed x15 -> x1, local copies, waits for them, and re-layouts: 7.02 us -> 3.05 us
    pallas_call x1, Pallas kernels: 98.4 us -> 96.2 us  [local(): pl.pallas_call(functools.partial(kernel, layers, groups), out_shape=jax.S...]
where the time goes in v2:
time: 99.4 us; the launch traced here: 99.2 us
  Pallas kernels  96.2 us (97%)
  local copies, waits for them, and re-layouts  3.05 us (3%)
    pallas_call x1, Pallas kernels, local(): pl.pallas_call(functools.partial(kernel, layers, groups), out_shape=jax.S...  96.2 us
    unnamed x1, local copies, waits for them, and re-layouts  3.05 us

profile of v2, /device:TPU:30, one launch (start us, length us, event | category | flops | bytes accessed | tf_op | source)
XLA Modules:
  0.0 99.2 jit_solution(9890122051393542844)
XLA Ops:
  0.0 96.2 %shard_map.82 = f32[4,512,256]{2,1,0:T(8,128)} custom-call(f32[1,256]{1,0:T(1,128)} %onsite.1, f32[1,256]{1,0:T(1,128)} %broad.1, f32[8]{0:T(128)} %weights.1, s32[8]{0:T(128)} %offsets.1, f32[512,256]{1,0:T(8,128)} %bitcast.7, f32[512,256]{1,0:T(8,128)} %bitcast.8, s32[256,256]{1,0:T(8,128)} %bitcast.9, f32[4,512,256]{2,1,0:T(8,128)} %bitcast.6), custom_call_target="tpu_custom_call" | custom-call | tf_op jit(solution)/shard_map/pallas_call | solution.py:433
  96.2 3.0 %copy.10 = f32[1,4,2,256,256]{4,3,2,1,0:T(8,128)} copy(f32[1,4,2,256,256]{4,3,2,1,0:T(8,128)} %bitcast.5) | data formatting | bytes 4194304

commit v3 on v2

--- a/solution.py
+++ b/solution.py
@@ -35,6 +35,20 @@
 
     yield three(re, re) - three(im, im)
     yield three(im, re) + three(re, im)
+
+
+def row_chunks(first, second, n, count=2):
+    fh, fl = first
+    sh, sl = second
+    re, im = slice(0, n), slice(n, 2 * n)
+
+    def three(rows, part):
+        return dot(fh[rows], sh[part]) + (dot(fl[rows], sh[part]) + dot(fh[rows], sl[part]))
+
+    size = n // count
+    for q in range(count):
+        top, low = slice(q * size, (q + 1) * size), slice(n + q * size, n + (q + 1) * size)
+        yield top, low, three(top, re) - three(low, im), three(low, re) + three(top, im)
 
 
 def kernel(
@@ -312,44 +326,50 @@
             to_next(t, 2).wait_recv()
             to_next(t, 3).wait_recv()
             keep(fourth, im, inc[t, im])
-            right = dot(ch[...], in_h[im]) + (dot(cl[...], in_h[im]) + dot(ch[...], in_l[im]))
-            way_real, way_imag = left[re] - right[im], left[im] + right[re]
-            keep(along, re, way_real)
-            keep(along, im, way_imag)
-            c_real, c_imag = coup_v[re], coup_v[im]
-            inverse = reciprocal(
-                diag_real - jnp.sum(way_real * c_real + way_imag * c_imag, axis=1, keepdims=True),
-                diag_imag - jnp.sum(way_imag * c_real - way_real * c_imag, axis=1, keepdims=True),
-            )
             size = n // 2
-            (ah, al), (dh, dl) = along, adjoint
+            diagonals = []
             for q in range(2):
                 top, low = slice(q * size, (q + 1) * size), slice(n + q * size, n + (q + 1) * size)
 
-                def three(rows, part):
-                    return dot(ah[rows], dh[part]) + (dot(al[rows], dh[part]) + dot(ah[rows], dl[part]))
-
-                real = three(top, re) - three(low, im) + contact[top]
-                imag = three(low, re) + three(top, im) + contact[low]
-                start_sweeps(q, size, real, imag, inverse)
-
-        for rows, part in zip((re, im), halves(residue, residue, n)):
-            keep(square, rows, part)
+                def right(rows):
+                    return dot(ch[rows], in_h[im]) + (dot(cl[rows], in_h[im]) + dot(ch[rows], in_l[im]))
+
+                way_real, way_imag = left[top] - right(low), left[low] + right(top)
+                keep(along, top, way_real)
+                keep(along, low, way_imag)
+                diagonals.append(
+                    (
+                        jnp.sum(way_real * coup_v[top] + way_imag * coup_v[low], axis=1, keepdims=True),
+                        jnp.sum(way_imag * coup_v[top] - way_real * coup_v[low], axis=1, keepdims=True),
+                    )
+                )
+            on_real, on_imag = (jnp.concatenate([d[i] for d in diagonals]) for i in range(2))
+            inverse = reciprocal(diag_real - on_real, diag_imag - on_imag)
+            for q, (top, low, real, imag) in enumerate(row_chunks(along, adjoint, n)):
+                start_sweeps(q, size, real + contact[top], imag + contact[low], inverse)
+
+        for top, low, real, imag in row_chunks(residue, residue, n):
+            keep(square, top, real)
+            keep(square, low, imag)
+        for top, low, real, imag in row_chunks(square, square, n):
+            keep(fourth, top, real)
+            keep(fourth, low, imag)
         for rows in (re, im):
             keep(first_sum, rows, one[rows])
-        for rows, part in zip((re, im), halves(first_sum, square, n)):
-            two[rows] = one[rows] + part
-            keep(second_sum, rows, two[rows])
-        for rows, part in zip((re, im), halves(square, square, n)):
-            keep(fourth, rows, part)
+        for top, low, real, imag in row_chunks(first_sum, square, n):
+            two[top] = one[top] + real
+            two[low] = one[low] + imag
+            keep(second_sum, top, two[top])
+            keep(second_sum, low, two[low])
         at_once = jnp.logical_and(has_next, jnp.logical_or(later_layer, t + odd == 0))
-        for parts, rows, part in zip(((0, 1), (2, 3)), (re, im), halves(second_sum, fourth, n)):
-            slots[7 + t, rows] = two[rows] + part
+        for q, (top, low, real, imag) in enumerate(row_chunks(second_sum, fourth, n)):
+            slots[7 + t, top] = two[top] + real
+            slots[7 + t, low] = two[low] + imag
 
             @pl.when(at_once)
             def _():
-                for p in parts:
-                    to_next(t, p).start()
+                to_next(t, q).start()
+                to_next(t, 2 + q).start()
 
         @pl.when(far_ok)
         def _():
@@ -466,17 +486,22 @@
                 pltpu.SemaphoreType.REGULAR,
             ],
             compiler_params=pltpu.CompilerParams(
-                collective_id=0, has_side_effects=True, vmem_limit_bytes=62 * 2**20
+                collective_id=0, has_side_effects=True, vmem_limit_bytes=50 * 2**20
             ),
         )(
-            onsite,
-            broad,
-            weights,
-            offsets,
-            ham.reshape(block),
-            coup.reshape(block),
-            mask.reshape(n, n),
-            prior.reshape(OWN, *block),
+            *(
+                pltpu.with_memory_space_constraint(v, pltpu.HBM)
+                for v in (
+                    onsite,
+                    broad,
+                    weights,
+                    offsets,
+                    ham.reshape(block),
+                    coup.reshape(block),
+                    mask.reshape(n, n),
+                    prior.reshape(OWN, *block),
+                )
+            ),
         )
         return result.reshape(1, OWN, 2, n, n)
 

time: 99.4 us -> 93.6 us (0.942)
  Pallas kernels: 96.2 us -> 92.1 us
  local copies, waits for them, and re-layouts: 3.05 us -> 1.32 us
    pallas_call x1, Pallas kernels: 96.2 us -> 92.1 us  [local(): pl.pallas_call(functools.partial(kernel, layers, groups), out_shape=jax.S...]
    unnamed x1, local copies, waits for them, and re-layouts: 3.05 us -> 1.32 us
where the time goes in v3:
time: 93.6 us; the launch traced here: 93.5 us
  Pallas kernels  92.1 us (98%)
  local copies, waits for them, and re-layouts  1.32 us (1%)
    pallas_call x1, Pallas kernels, local(): pl.pallas_call(functools.partial(kernel, layers, groups), out_shape=jax.S...  92.1 us

profile of v3, /device:TPU:30, one launch (start us, length us, event | category | flops | bytes accessed | tf_op | source)
XLA Modules:
  0.0 93.5 jit_solution(14882178511271313544)
XLA Ops:
  0.0 92.1 %shard_map.82 = f32[4,512,256]{2,1,0:T(8,128)S(1)} custom-call(f32[1,256]{1,0:T(1,128)} %onsite.1, f32[1,256]{1,0:T(1,128)} %broad.1, f32[8]{0:T(128)} %weights.1, s32[8]{0:T(128)} %offsets.1, f32[512,256]{1,0:T(8,128)} %bitcast.7, f32[512,256]{1,0:T(8,128)} %bitcast.8, s32[256,256]{1,0:T(8,128)} %bitcast.9, f32[4,512,256]{2,1,0:T(8,128)} %bitcast.6), custom_call_target="tpu_custom_call" | custom-call | tf_op jit(solution)/shard_map/pallas_call | solution.py:453
  92.1 1.3 %copy.10 = f32[1,4,2,256,256]{4,3,2,1,0:T(8,128)} copy(f32[1,4,2,256,256]{4,3,2,1,0:T(8,128)S(1)} %bitcast.5) | data formatting | bytes 4194304

commit v4 on v3

--- a/solution.py
+++ b/solution.py
@@ -78,6 +78,9 @@
     contact,
     one,
     two,
+    again_base,
+    again_coup,
+    again_prior,
     pairs,
     table,
     load_sem,
@@ -89,7 +92,15 @@
     skip_sem,
     fwd_sem,
     slot_sem,
-    out_sem,
+    last_send,
+    last_recv,
+    twice_sem,
+    const_send,
+    const_recv,
+    share_send,
+    share_recv,
+    again_send,
+    again_recv,
     token,
 ):
     n = onsite.shape[-1]
@@ -105,11 +116,15 @@
     far_ok = jnp.logical_and(far >= 0, far < groups)
     first_layer = x == 0
     later_layer = x > 0
-    has_next = x < layers - 1
+    has_next = x < layers - 2
+    sends_twice = x == layers - 3
+    constants_on = x == layers - 2
+    last_layer = x == layers - 1
     re, im = slice(0, n), slice(n, 2 * n)
     coupled, adjoint, along, residue, square, first_sum, fourth, second_sum = (
         (pairs.at[2 * i], pairs.at[2 * i + 1]) for i in range(8)
     )
+    again_coupled, again_adjoint = ((pairs.at[2 * i], pairs.at[2 * i + 1]) for i in (8, 9))
 
     def keep(pair, rows, value):
         pair[0][rows], pair[1][rows] = split(value)
@@ -154,6 +169,10 @@
     def _():
         pl.semaphore_signal(barrier, inc=1, device_id=(x - 1, m), device_id_type=MESH)
 
+    @pl.when(last_layer)
+    def _():
+        pl.semaphore_signal(barrier, inc=1, device_id=(layers - 3, m), device_id_type=MESH)
+
     def prepare():
         acc[...] = jnp.zeros_like(acc)
 
@@ -178,15 +197,19 @@
     kept = mask_v[...].astype(F32)
     coup_v[re] = coup_v[re] * kept
     coup_v[im] = coup_v[im] * kept
-    keep(coupled, re, coup_v[re])
-    keep(coupled, im, coup_v[im])
-    keep(adjoint, re, coup_v[re].T)
-    keep(adjoint, im, -coup_v[im].T)
-    loads[2].wait()
-    base[re] = 0.5 * (ham_v[re] + ham_v[re].T)
-    base[im] = 0.5 * (ham_v[im] - ham_v[im].T)
-    loads[3].wait()
-    loads[4].wait()
+
+    def factors(source, left, right):
+        keep(left, re, source[re])
+        keep(left, im, source[im])
+        keep(right, re, source[re].T)
+        keep(right, im, -source[im].T)
+
+    factors(coup_v, coupled, adjoint)
+    for load in loads[2:5]:
+        load.wait()
+    eye = lax.broadcasted_iota(jnp.int32, (n, n), 0) == lax.broadcasted_iota(jnp.int32, (n, n), 1)
+    base[re] = 0.5 * (ham_v[re] + ham_v[re].T) + jnp.where(eye, onsite_v[...], 0.0)
+    base[im] = 0.5 * (ham_v[im] - ham_v[im].T) - jnp.where(eye, broad_v[...], 0.0)
 
     @pl.when(first_layer)
     def _():
@@ -201,8 +224,58 @@
 
     pl.semaphore_wait(
         barrier,
-        1 + far_ok.astype(jnp.int32) + near_ok.astype(jnp.int32) + has_next.astype(jnp.int32),
+        1
+        + far_ok.astype(jnp.int32)
+        + near_ok.astype(jnp.int32)
+        + (x < layers - 1).astype(jnp.int32)
+        + sends_twice.astype(jnp.int32),
     )
+
+    def remote(source, target, send_sem, recv_sem, device):
+        return pltpu.make_async_remote_copy(
+            src_ref=source,
+            dst_ref=target,
+            send_sem=send_sem,
+            recv_sem=recv_sem,
+            device_id=device,
+            device_id_type=MESH,
+        )
+
+    own_half = pl.ds(pl.multiple_of(odd * n, n), n)
+    other_half = pl.ds(pl.multiple_of((1 - odd) * n, n), n)
+
+    def constants(i):
+        return remote(
+            (coup_v, base)[i].at[own_half],
+            (again_coup, again_base)[i].at[own_half],
+            const_send.at[i],
+            const_recv.at[i],
+            (layers - 1, m),
+        )
+
+    def share(i, half):
+        ref = (again_coup, again_base)[i].at[half]
+        return remote(ref, ref, share_send.at[i], share_recv.at[i], (x, near))
+
+    def prior_on(t):
+        return remote(prior_v.at[t], again_prior.at[t], again_send.at[t], again_recv.at[t], (layers - 1, m))
+
+    @pl.when(constants_on)
+    def _():
+        constants(0).start()
+        constants(1).start()
+        for t in range(OWN):
+            prior_load(t).wait()
+            prior_on(t).start()
+
+    @pl.when(last_layer)
+    def _():
+        for i in range(2):
+            constants(i).wait_recv()
+            share(i, own_half).start()
+        for i in range(2):
+            share(i, other_half).wait_recv()
+        factors(again_coup, again_coupled, again_adjoint)
 
     quarter = n // 2
 
@@ -217,6 +290,16 @@
             device_id_type=MESH,
         )
 
+    def to_last(t, part):
+        rows = pl.ds(part * quarter, quarter)
+        return remote(
+            slots.at[7 + t, rows],
+            inc.at[t, rows],
+            twice_sem.at[t, part],
+            xr_sem.at[t, part],
+            (layers - 1, m),
+        )
+
     def send(source, target, send_sem, device):
         return pltpu.make_async_remote_copy(
             src_ref=slots.at[source],
@@ -233,6 +316,23 @@
     def to_far(t):
         return send(7 + t, 6 - t, far_sem.at[t], far)
 
+    def last_step(part, target, i, device):
+        rows = pl.ds(part * quarter, quarter)
+        return pltpu.make_async_remote_copy(
+            src_ref=slots.at[7 + OWN - 1, rows],
+            dst_ref=slots.at[target, rows],
+            send_sem=last_send.at[i, part],
+            recv_sem=last_recv.at[i, part],
+            device_id=(x, device),
+            device_id_type=MESH,
+        )
+
+    def last_to_far(part):
+        return last_step(part, 6 - (OWN - 1), 0, far)
+
+    def last_to_skip(part):
+        return last_step(part, OWN - 2, 1, skip)
+
     def to_skip(t):
         return send(7 + t, t - 1, skip_sem.at[t], skip)
 
@@ -242,7 +342,7 @@
     def arrived(slot):
         send(slot, slot, near_sem.at[0], near).wait_recv()
 
-    def accumulate(sources):
+    def accumulate(sources, first=0, last=2 * n, final=False):
         taps = [[table[u - v + 3] for v in range(OWN)] for u in sources]
 
         def body(c, carry):
@@ -252,19 +352,19 @@
                 total = acc[v, rows, :]
                 for s in range(len(sources)):
                     total = total + taps[s][v] * blocks[s]
-                acc[v, rows, :] = total
+                if final:
+                    out[place(v), rows, :] = total
+                else:
+                    acc[v, rows, :] = total
             return carry
 
-        lax.fori_loop(0, 2 * n // 16, body, 0)
+        lax.fori_loop(first // 16, last // 16, body, 0)
 
     def gather(t):
         @pl.when(far_ok)
         def _():
             arrived(6 - t)
-
-            @pl.when(t < OWN - 1)
-            def _():
-                forward(t).start()
+            forward(t).start()
 
         arrived(14 - t)
         accumulate([7 + t, 14 - t, 6 - t])
@@ -280,8 +380,6 @@
                 arrived(14 + t)
 
             accumulate([t - 1, 14 + t])
-
-    eye = lax.broadcasted_iota(jnp.int32, (n, n), 0) == lax.broadcasted_iota(jnp.int32, (n, n), 1)
 
     def reciprocal(diag_real, diag_imag):
         modulus = diag_real * diag_real + diag_imag * diag_imag
@@ -304,50 +402,43 @@
         one[q * size : (q + 1) * size] = jnp.where(on, row_real, cr * res_real - ci * res_imag)
         one[n + q * size : n + (q + 1) * size] = jnp.where(on, row_imag, cr * res_imag + ci * res_real)
 
-    def step(t, carry):
-        prior_load(t).wait()
-        energy = (m * OWN + place(t)).astype(F32)
-        level = -1.0 + 2.0 * (energy + 0.5) / (groups * OWN)
-        contact[...] = base[...] + prior_v[t]
-        diag_real = jnp.sum(jnp.where(eye, (level - onsite_v[...]) - contact[re], 0.0), axis=1, keepdims=True)
-        diag_imag = jnp.sum(jnp.where(eye, broad_v[...] - contact[im], 0.0), axis=1, keepdims=True)
-
-        @pl.when(first_layer)
-        def _():
-            start_sweeps(0, n, contact[re], contact[im], reciprocal(diag_real, diag_imag))
-
-        @pl.when(later_layer)
-        def _():
-            to_next(t, 0).wait_recv()
-            to_next(t, 1).wait_recv()
-            (ch, cl), (in_h, in_l) = coupled, fourth
-            keep(fourth, re, inc[t, re])
-            left = dot(ch[...], in_h[re]) + (dot(cl[...], in_h[re]) + dot(ch[...], in_l[re]))
-            to_next(t, 2).wait_recv()
-            to_next(t, 3).wait_recv()
-            keep(fourth, im, inc[t, im])
-            size = n // 2
-            diagonals = []
-            for q in range(2):
-                top, low = slice(q * size, (q + 1) * size), slice(n + q * size, n + (q + 1) * size)
-
-                def right(rows):
-                    return dot(ch[rows], in_h[im]) + (dot(cl[rows], in_h[im]) + dot(ch[rows], in_l[im]))
-
-                way_real, way_imag = left[top] - right(low), left[low] + right(top)
-                keep(along, top, way_real)
-                keep(along, low, way_imag)
-                diagonals.append(
-                    (
-                        jnp.sum(way_real * coup_v[top] + way_imag * coup_v[low], axis=1, keepdims=True),
-                        jnp.sum(way_imag * coup_v[top] - way_real * coup_v[low], axis=1, keepdims=True),
-                    )
+    def diagonal(level):
+        return (
+            jnp.sum(jnp.where(eye, level - contact[re], 0.0), axis=1, keepdims=True),
+            jnp.sum(jnp.where(eye, -contact[im], 0.0), axis=1, keepdims=True),
+        )
+
+    def meet(arriving, wait, left_pair, right_pair, coup_ref, diag):
+        diag_real, diag_imag = diag
+        wait(0, 1)
+        (ch, cl), (in_h, in_l) = left_pair, fourth
+        keep(fourth, re, arriving[re])
+        left = dot(ch[...], in_h[re]) + (dot(cl[...], in_h[re]) + dot(ch[...], in_l[re]))
+        wait(2, 3)
+        keep(fourth, im, arriving[im])
+        size = n // 2
+        diagonals = []
+        for q in range(2):
+            top, low = slice(q * size, (q + 1) * size), slice(n + q * size, n + (q + 1) * size)
+
+            def right(rows):
+                return dot(ch[rows], in_h[im]) + (dot(cl[rows], in_h[im]) + dot(ch[rows], in_l[im]))
+
+            way_real, way_imag = left[top] - right(low), left[low] + right(top)
+            keep(along, top, way_real)
+            keep(along, low, way_imag)
+            diagonals.append(
+                (
+                    jnp.sum(way_real * coup_ref[top] + way_imag * coup_ref[low], axis=1, keepdims=True),
+                    jnp.sum(way_imag * coup_ref[top] - way_real * coup_ref[low], axis=1, keepdims=True),
                 )
-            on_real, on_imag = (jnp.concatenate([d[i] for d in diagonals]) for i in range(2))
-            inverse = reciprocal(diag_real - on_real, diag_imag - on_imag)
-            for q, (top, low, real, imag) in enumerate(row_chunks(along, adjoint, n)):
-                start_sweeps(q, size, real + contact[top], imag + contact[low], inverse)
-
+            )
+        on_real, on_imag = (jnp.concatenate([d[i] for d in diagonals]) for i in range(2))
+        inverse = reciprocal(diag_real - on_real, diag_imag - on_imag)
+        for q, (top, low, real, imag) in enumerate(row_chunks(along, right_pair, n)):
+            start_sweeps(q, size, real + contact[top], imag + contact[low], inverse)
+
+    def sweeps():
         for top, low, real, imag in row_chunks(residue, residue, n):
             keep(square, top, real)
             keep(square, low, imag)
@@ -361,21 +452,76 @@
             two[low] = one[low] + imag
             keep(second_sum, top, two[top])
             keep(second_sum, low, two[low])
+        for top, low, real, imag in row_chunks(second_sum, fourth, n):
+            yield top, low, two[top] + real, two[low] + imag
+
+    def step(t, carry):
+        @pl.when(jnp.logical_not(constants_on))
+        def _():
+            prior_load(t).wait()
+
+        energy = (m * OWN + place(t)).astype(F32)
+        level = -1.0 + 2.0 * (energy + 0.5) / (groups * OWN)
+
+        def come(*parts):
+            for p in parts:
+                to_next(t, p).wait_recv()
+
+        @pl.when(last_layer)
+        def _():
+            prior_on(t).wait_recv()
+            contact[...] = again_base[...] + again_prior[t]
+            meet(inc.at[t], come, again_coupled, again_adjoint, again_coup, diagonal(level))
+            for top, low, real, imag in sweeps():
+                inc[t, top] = real
+                inc[t, low] = imag
+
+        contact[...] = base[...] + prior_v[t]
+        diag = diagonal(level)
+
+        @pl.when(first_layer)
+        def _():
+            start_sweeps(0, n, contact[re], contact[im], reciprocal(*diag))
+
+        def come_here(*parts):
+            @pl.when(jnp.logical_not(last_layer))
+            def _():
+                come(*parts)
+
+        @pl.when(later_layer)
+        def _():
+            meet(inc.at[t], come_here, coupled, adjoint, coup_v, diag)
+
         at_once = jnp.logical_and(has_next, jnp.logical_or(later_layer, t + odd == 0))
-        for q, (top, low, real, imag) in enumerate(row_chunks(second_sum, fourth, n)):
-            slots[7 + t, top] = two[top] + real
-            slots[7 + t, low] = two[low] + imag
+        for q, (top, low, real, imag) in enumerate(sweeps()):
+            slots[7 + t, top] = real
+            slots[7 + t, low] = imag
 
             @pl.when(at_once)
             def _():
                 to_next(t, q).start()
                 to_next(t, 2 + q).start()
 
-        @pl.when(far_ok)
+            @pl.when(sends_twice)
+            def _():
+                to_last(t, q).start()
+                to_last(t, 2 + q).start()
+
+            @pl.when(jnp.logical_and(far_ok, t == OWN - 1))
+            def _():
+                last_to_far(q).start()
+                last_to_far(2 + q).start()
+
+            @pl.when(jnp.logical_and(near_ok, t == OWN - 1))
+            def _():
+                last_to_skip(q).start()
+                last_to_skip(2 + q).start()
+
+        @pl.when(jnp.logical_and(far_ok, t < OWN - 1))
         def _():
             to_far(t).start()
 
-        @pl.when(jnp.logical_and(near_ok, t > 0))
+        @pl.when(jnp.logical_and(near_ok, jnp.logical_and(t > 0, t < OWN - 1)))
         def _():
             to_skip(t).start()
 
@@ -407,13 +553,30 @@
         return carry
 
     lax.fori_loop(0, OWN, step, 0)
-    gather(OWN - 1)
-
-    stores = [
-        pltpu.make_async_copy(acc.at[v], out.at[place(v)], out_sem.at[v]) for v in range(OWN)
-    ]
-    for store in stores:
-        store.start()
+    t = OWN - 1
+    @pl.when(near_ok)
+    def _():
+        arrived(14 + t)
+
+    arrived(14 - t)
+    accumulate([14 + t, 7 + t, 14 - t])
+    for part in (0, 2, 1, 3):
+
+        @pl.when(far_ok)
+        def _():
+            last_to_far(part).wait_recv()
+            last_to_skip(part).wait_recv()
+
+        accumulate([6 - t, t - 1], part * quarter, (part + 1) * quarter, final=True)
+    for i in range(2):
+
+        @pl.when(constants_on)
+        def _():
+            constants(i).wait_send()
+
+        @pl.when(last_layer)
+        def _():
+            share(i, own_half).wait_send()
 
     for t in range(OWN):
         to_near(t).wait_send()
@@ -427,20 +590,33 @@
 
             to_next(t, 3).wait_send()
 
+        @pl.when(sends_twice)
+        def _():
+            for p in range(4):
+                to_last(t, p).wait_send()
+
+        @pl.when(constants_on)
+        def _():
+            prior_on(t).wait_send()
+
         @pl.when(far_ok)
         def _():
-            to_far(t).wait_send()
             if t < OWN - 1:
+                to_far(t).wait_send()
                 forward(t).wait_send()
+            else:
+                for part in range(4):
+                    last_to_far(part).wait_send()
 
         if t > 0:
 
             @pl.when(near_ok)
             def _():
-                to_skip(t).wait_send()
-
-    for store in stores:
-        store.wait()
+                if t < OWN - 1:
+                    to_skip(t).wait_send()
+                else:
+                    for part in range(4):
+                        last_to_skip(part).wait_send()
 
 
 def solution(mesh):
@@ -454,7 +630,7 @@
             functools.partial(kernel, layers, groups),
             out_shape=jax.ShapeDtypeStruct((OWN, 2 * n, n), F32),
             in_specs=[hbm] * 8,
-            out_specs=hbm,
+            out_specs=pl.BlockSpec(memory_space=pltpu.VMEM),
             scratch_shapes=[
                 pltpu.VMEM((1, n), F32),
                 pltpu.VMEM((1, n), F32),
@@ -471,7 +647,10 @@
                 pltpu.VMEM(block, F32),
                 pltpu.VMEM(block, F32),
                 pltpu.VMEM(block, F32),
-                pltpu.VMEM((16, *block), BF16),
+                pltpu.VMEM(block, F32),
+                pltpu.VMEM(block, F32),
+                pltpu.VMEM((OWN, *block), F32),
+                pltpu.VMEM((20, *block), BF16),
                 pltpu.SMEM((SLOTS + 3,), F32),
                 pltpu.SemaphoreType.DMA((7,)),
                 pltpu.SemaphoreType.DMA((OWN,)),
@@ -482,6 +661,14 @@
                 pltpu.SemaphoreType.DMA((OWN,)),
                 pltpu.SemaphoreType.DMA((OWN,)),
                 pltpu.SemaphoreType.DMA((SLOTS,)),
+                pltpu.SemaphoreType.DMA((2, 4)),
+                pltpu.SemaphoreType.DMA((2, 4)),
+                pltpu.SemaphoreType.DMA((OWN, 4)),
+                pltpu.SemaphoreType.DMA((2,)),
+                pltpu.SemaphoreType.DMA((2,)),
+                pltpu.SemaphoreType.DMA((2,)),
+                pltpu.SemaphoreType.DMA((2,)),
+                pltpu.SemaphoreType.DMA((OWN,)),
                 pltpu.SemaphoreType.DMA((OWN,)),
                 pltpu.SemaphoreType.REGULAR,
             ],

time: 93.6 us -> 87.6 us (0.936)
  Pallas kernels: 92.1 us -> 86.2 us
    pallas_call x1, Pallas kernels: 92.1 us -> 86.2 us  [local(): pl.pallas_call(functools.partial(kernel, layers, groups), out_shape=jax.S...]
where the time goes in v4:
time: 87.6 us; the launch traced here: 87.5 us
  Pallas kernels  86.2 us (98%)
  local copies, waits for them, and re-layouts  1.32 us (2%)
    pallas_call x1, Pallas kernels, local(): pl.pallas_call(functools.partial(kernel, layers, groups), out_shape=jax.S...  86.2 us

profile of v4, /device:TPU:30, one launch (start us, length us, event | category | flops | bytes accessed | tf_op | source)
XLA Modules:
  0.0 87.5 jit_solution(14774395945616739445)
XLA Ops:
  0.0 86.2 %shard_map.82 = f32[4,512,256]{2,1,0:T(8,128)S(1)} custom-call(f32[1,256]{1,0:T(1,128)} %onsite.1, f32[1,256]{1,0:T(1,128)} %broad.1, f32[8]{0:T(128)} %weights.1, s32[8]{0:T(128)} %offsets.1, f32[512,256]{1,0:T(8,128)} %bitcast.7, f32[512,256]{1,0:T(8,128)} %bitcast.8, s32[256,256]{1,0:T(8,128)} %bitcast.9, f32[4,512,256]{2,1,0:T(8,128)} %bitcast.6), custom_call_target="tpu_custom_call" | custom-call | tf_op jit(solution)/shard_map/pallas_call | solution.py:629
  86.2 1.3 %copy.10 = f32[1,4,2,256,256]{4,3,2,1,0:T(8,128)} copy(f32[1,4,2,256,256]{4,3,2,1,0:T(8,128)S(1)} %bitcast.5) | data formatting | bytes 4194304

commit v5 on v4

--- a/solution.py
+++ b/solution.py
@@ -78,7 +78,6 @@
     contact,
     one,
     two,
-    again_base,
     again_coup,
     again_prior,
     pairs,
@@ -244,37 +243,32 @@
     own_half = pl.ds(pl.multiple_of(odd * n, n), n)
     other_half = pl.ds(pl.multiple_of((1 - odd) * n, n), n)
 
-    def constants(i):
-        return remote(
-            (coup_v, base)[i].at[own_half],
-            (again_coup, again_base)[i].at[own_half],
-            const_send.at[i],
-            const_recv.at[i],
-            (layers - 1, m),
-        )
-
-    def share(i, half):
-        ref = (again_coup, again_base)[i].at[half]
-        return remote(ref, ref, share_send.at[i], share_recv.at[i], (x, near))
+    def constants():
+        return remote(coup_v.at[own_half], again_coup.at[own_half], const_send, const_recv, (layers - 1, m))
+
+    def share(half):
+        ref = again_coup.at[half]
+        return remote(ref, ref, share_send, share_recv, (x, near))
 
     def prior_on(t):
         return remote(prior_v.at[t], again_prior.at[t], again_send.at[t], again_recv.at[t], (layers - 1, m))
 
     @pl.when(constants_on)
     def _():
-        constants(0).start()
-        constants(1).start()
+        constants().start()
         for t in range(OWN):
             prior_load(t).wait()
-            prior_on(t).start()
+            prior_v[t] = prior_v[t] + base[...]
+        constants().wait_send()
+        prior_on(0).start()
+        prior_on(0).wait_send()
+        prior_on(1).start()
 
     @pl.when(last_layer)
     def _():
-        for i in range(2):
-            constants(i).wait_recv()
-            share(i, own_half).start()
-        for i in range(2):
-            share(i, other_half).wait_recv()
+        constants().wait_recv()
+        share(own_half).start()
+        share(other_half).wait_recv()
         factors(again_coup, again_coupled, again_adjoint)
 
     quarter = n // 2
@@ -399,8 +393,12 @@
         keep(residue, rows, res_real)
         keep(residue, slice(n + q * size, n + (q + 1) * size), res_imag)
         cr, ci = col_real[rows], col_imag[rows]
-        one[q * size : (q + 1) * size] = jnp.where(on, row_real, cr * res_real - ci * res_imag)
-        one[n + q * size : n + (q + 1) * size] = jnp.where(on, row_imag, cr * res_imag + ci * res_real)
+        one_real = jnp.where(on, row_real, cr * res_real - ci * res_imag)
+        one_imag = jnp.where(on, row_imag, cr * res_imag + ci * res_real)
+        low = slice(n + q * size, n + (q + 1) * size)
+        one[rows], one[low] = one_real, one_imag
+        keep(first_sum, rows, one_real)
+        keep(first_sum, low, one_imag)
 
     def diagonal(level):
         return (
@@ -445,8 +443,6 @@
         for top, low, real, imag in row_chunks(square, square, n):
             keep(fourth, top, real)
             keep(fourth, low, imag)
-        for rows in (re, im):
-            keep(first_sum, rows, one[rows])
         for top, low, real, imag in row_chunks(first_sum, square, n):
             two[top] = one[top] + real
             two[low] = one[low] + imag
@@ -470,13 +466,20 @@
         @pl.when(last_layer)
         def _():
             prior_on(t).wait_recv()
-            contact[...] = again_base[...] + again_prior[t]
+            contact[...] = again_prior[t]
             meet(inc.at[t], come, again_coupled, again_adjoint, again_coup, diagonal(level))
             for top, low, real, imag in sweeps():
                 inc[t, top] = real
                 inc[t, low] = imag
 
-        contact[...] = base[...] + prior_v[t]
+        @pl.when(constants_on)
+        def _():
+            contact[...] = prior_v[t]
+
+        @pl.when(jnp.logical_not(constants_on))
+        def _():
+            contact[...] = base[...] + prior_v[t]
+
         diag = diagonal(level)
 
         @pl.when(first_layer)
@@ -497,16 +500,16 @@
             slots[7 + t, top] = real
             slots[7 + t, low] = imag
 
+            @pl.when(sends_twice)
+            def _():
+                to_last(t, q).start()
+                to_last(t, 2 + q).start()
+
             @pl.when(at_once)
             def _():
                 to_next(t, q).start()
                 to_next(t, 2 + q).start()
 
-            @pl.when(sends_twice)
-            def _():
-                to_last(t, q).start()
-                to_last(t, 2 + q).start()
-
             @pl.when(jnp.logical_and(far_ok, t == OWN - 1))
             def _():
                 last_to_far(q).start()
@@ -526,6 +529,11 @@
             to_skip(t).start()
 
         to_near(t).start()
+
+        @pl.when(jnp.logical_and(constants_on, t < OWN - 2))
+        def _():
+            prior_on(t + 1).wait_send()
+            prior_on(t + 2).start()
 
         @pl.when(jnp.logical_and(first_layer, t + odd > 0))
         def _():
@@ -568,15 +576,13 @@
             last_to_skip(part).wait_recv()
 
         accumulate([6 - t, t - 1], part * quarter, (part + 1) * quarter, final=True)
-    for i in range(2):
-
-        @pl.when(constants_on)
-        def _():
-            constants(i).wait_send()
-
-        @pl.when(last_layer)
-        def _():
-            share(i, own_half).wait_send()
+    @pl.when(constants_on)
+    def _():
+        prior_on(OWN - 1).wait_send()
+
+    @pl.when(last_layer)
+    def _():
+        share(own_half).wait_send()
 
     for t in range(OWN):
         to_near(t).wait_send()
@@ -594,10 +600,6 @@
         def _():
             for p in range(4):
                 to_last(t, p).wait_send()
-
-        @pl.when(constants_on)
-        def _():
-            prior_on(t).wait_send()
 
         @pl.when(far_ok)
         def _():
@@ -648,7 +650,6 @@
                 pltpu.VMEM(block, F32),
                 pltpu.VMEM(block, F32),
                 pltpu.VMEM(block, F32),
-                pltpu.VMEM(block, F32),
                 pltpu.VMEM((OWN, *block), F32),
                 pltpu.VMEM((20, *block), BF16),
                 pltpu.SMEM((SLOTS + 3,), F32),
@@ -664,10 +665,10 @@
                 pltpu.SemaphoreType.DMA((2, 4)),
                 pltpu.SemaphoreType.DMA((2, 4)),
                 pltpu.SemaphoreType.DMA((OWN, 4)),
-                pltpu.SemaphoreType.DMA((2,)),
-                pltpu.SemaphoreType.DMA((2,)),
-                pltpu.SemaphoreType.DMA((2,)),
-                pltpu.SemaphoreType.DMA((2,)),
+                pltpu.SemaphoreType.DMA,
+                pltpu.SemaphoreType.DMA,
+                pltpu.SemaphoreType.DMA,
+                pltpu.SemaphoreType.DMA,
                 pltpu.SemaphoreType.DMA((OWN,)),
                 pltpu.SemaphoreType.DMA((OWN,)),
                 pltpu.SemaphoreType.REGULAR,

time: 87.6 us -> 85.3 us (0.974)
  Pallas kernels: 86.2 us -> 83.9 us
    pallas_call x1, Pallas kernels: 86.2 us -> 83.9 us  [local(): pl.pallas_call(functools.partial(kernel, layers, groups), out_shape=jax.S...]
where the time goes in v5:
time: 85.3 us; the launch traced here: 85.2 us
  Pallas kernels  83.9 us (98%)
  local copies, waits for them, and re-layouts  1.32 us (2%)
    pallas_call x1, Pallas kernels, local(): pl.pallas_call(functools.partial(kernel, layers, groups), out_shape=jax.S...  83.9 us

profile of v5, /device:TPU:30, one launch (start us, length us, event | category | flops | bytes accessed | tf_op | source)
XLA Modules:
  0.0 85.2 jit_solution(14863268770899784060)
XLA Ops:
  0.0 83.9 %shard_map.82 = f32[4,512,256]{2,1,0:T(8,128)S(1)} custom-call(f32[1,256]{1,0:T(1,128)} %onsite.1, f32[1,256]{1,0:T(1,128)} %broad.1, f32[8]{0:T(128)} %weights.1, s32[8]{0:T(128)} %offsets.1, f32[512,256]{1,0:T(8,128)} %bitcast.7, f32[512,256]{1,0:T(8,128)} %bitcast.8, s32[256,256]{1,0:T(8,128)} %bitcast.9, f32[4,512,256]{2,1,0:T(8,128)} %bitcast.6), custom_call_target="tpu_custom_call" | custom-call | tf_op jit(solution)/shard_map/pallas_call | solution.py:631
  83.9 1.3 %copy.10 = f32[1,4,2,256,256]{4,3,2,1,0:T(8,128)} copy(f32[1,4,2,256,256]{4,3,2,1,0:T(8,128)S(1)} %bitcast.5) | data formatting | bytes 4194304

commit v6 on v5

--- a/solution.py
+++ b/solution.py
@@ -400,13 +400,13 @@
         keep(first_sum, rows, one_real)
         keep(first_sum, low, one_imag)
 
-    def diagonal(level):
+    def diagonal(level, rest):
         return (
-            jnp.sum(jnp.where(eye, level - contact[re], 0.0), axis=1, keepdims=True),
-            jnp.sum(jnp.where(eye, -contact[im], 0.0), axis=1, keepdims=True),
+            jnp.sum(jnp.where(eye, level - rest[re], 0.0), axis=1, keepdims=True),
+            jnp.sum(jnp.where(eye, -rest[im], 0.0), axis=1, keepdims=True),
         )
 
-    def meet(arriving, wait, left_pair, right_pair, coup_ref, diag):
+    def meet(arriving, wait, left_pair, right_pair, coup_ref, rest, diag):
         diag_real, diag_imag = diag
         wait(0, 1)
         (ch, cl), (in_h, in_l) = left_pair, fourth
@@ -434,7 +434,7 @@
         on_real, on_imag = (jnp.concatenate([d[i] for d in diagonals]) for i in range(2))
         inverse = reciprocal(diag_real - on_real, diag_imag - on_imag)
         for q, (top, low, real, imag) in enumerate(row_chunks(along, right_pair, n)):
-            start_sweeps(q, size, real + contact[top], imag + contact[low], inverse)
+            start_sweeps(q, size, real + rest[top], imag + rest[low], inverse)
 
     def sweeps():
         for top, low, real, imag in row_chunks(residue, residue, n):
@@ -463,25 +463,25 @@
             for p in parts:
                 to_next(t, p).wait_recv()
 
+        @pl.when(constants_on)
+        def _():
+            contact[...] = prior_v[t]
+
+        @pl.when(jnp.logical_not(constants_on))
+        def _():
+            contact[...] = base[...] + prior_v[t]
+
+        diag = diagonal(level, contact)
+
         @pl.when(last_layer)
         def _():
             prior_on(t).wait_recv()
-            contact[...] = again_prior[t]
-            meet(inc.at[t], come, again_coupled, again_adjoint, again_coup, diagonal(level))
+            rest = again_prior.at[t]
+            meet(inc.at[t], come, again_coupled, again_adjoint, again_coup, rest, diagonal(level, rest))
             for top, low, real, imag in sweeps():
                 inc[t, top] = real
                 inc[t, low] = imag
 
-        @pl.when(constants_on)
-        def _():
-            contact[...] = prior_v[t]
-
-        @pl.when(jnp.logical_not(constants_on))
-        def _():
-            contact[...] = base[...] + prior_v[t]
-
-        diag = diagonal(level)
-
         @pl.when(first_layer)
         def _():
             start_sweeps(0, n, contact[re], contact[im], reciprocal(*diag))
@@ -493,7 +493,7 @@
 
         @pl.when(later_layer)
         def _():
-            meet(inc.at[t], come_here, coupled, adjoint, coup_v, diag)
+            meet(inc.at[t], come_here, coupled, adjoint, coup_v, contact, diag)
 
         at_once = jnp.logical_and(has_next, jnp.logical_or(later_layer, t + odd == 0))
         for q, (top, low, real, imag) in enumerate(sweeps()):

time: 85.3 us -> 85.1 us (level)
  no operation moved by 1% of the time
where the time goes in v6:
time: 85.1 us; the launch traced here: 85 us
  Pallas kernels  83.7 us (98%)
  local copies, waits for them, and re-layouts  1.32 us (2%)
    pallas_call x1, Pallas kernels, local(): pl.pallas_call(functools.partial(kernel, layers, groups), out_shape=jax.S...  83.7 us

profile of v6, /device:TPU:30, one launch (start us, length us, event | category | flops | bytes accessed | tf_op | source)
XLA Modules:
  0.0 85.0 jit_solution(8841241353711082631)
XLA Ops:
  0.0 83.7 %shard_map.82 = f32[4,512,256]{2,1,0:T(8,128)S(1)} custom-call(f32[1,256]{1,0:T(1,128)} %onsite.1, f32[1,256]{1,0:T(1,128)} %broad.1, f32[8]{0:T(128)} %weights.1, s32[8]{0:T(128)} %offsets.1, f32[512,256]{1,0:T(8,128)} %bitcast.7, f32[512,256]{1,0:T(8,128)} %bitcast.8, s32[256,256]{1,0:T(8,128)} %bitcast.9, f32[4,512,256]{2,1,0:T(8,128)} %bitcast.6), custom_call_target="tpu_custom_call" | custom-call | tf_op jit(solution)/shard_map/pallas_call | solution.py:631
  83.7 1.3 %copy.10 = f32[1,4,2,256,256]{4,3,2,1,0:T(8,128)} copy(f32[1,4,2,256,256]{4,3,2,1,0:T(8,128)S(1)} %bitcast.5) | data formatting | bytes 4194304
